TPU v7x, 512 devices: a whole 4x4x16 slice. The times are simulated.
512 devices in a mesh: gx: 32 (over z, x_hi), gy: 16 (over y, x_lo, core).
Axes of the slice: x: 4 (x_hi: 2, x_lo: 2; x = x_hi * 2 + x_lo), y: 4, z: 16, core: 2. Of those that a mesh axis runs over, the one named last changes fastest.
Arguments:
- tokens: bfloat16 [512, 16384], P('gy', 'gx'), may hold values from -320 to 320
- gate_weight: bfloat16 [16384, 26624], P('gx', 'gy'), may hold values from -0.046875 to 0.046875
- up_weight: bfloat16 [16384, 26624], P('gx', 'gy'), may hold values from -0.046875 to 0.046875
- down_weight: bfloat16 [26624, 16384], P('gy', 'gx'), may hold values from -0.0390625 to 0.0390625
- sign_bits: int32 [26624], P('gy'), may hold values from 0 to 1
Outputs:
- block_out: bfloat16 [512, 16384], P('gy', 'gx')
All inputs are finite; a program needn't handle non-finite values.
Results may differ from a plain program's by a relative error of at most 0.034.
Values may be sent and summed in bfloat16 or wider, within the bound.
No kernel may reach another device: no remote copies, remote signals or barrier semaphores. Data moves between devices by JAX's collectives and lax.ppermute only.
A program may use at most 64 MiB of HBM per device.

v0:
```python
import jax
import jax.numpy as jnp
from jax import lax
from jax.sharding import PartitionSpec as P

D = 16384
HAD = 128


epsilon = 1e-05


def hadamard():
    row_index = jnp.arange(HAD, dtype=jnp.int32)[:, None]
    col_index = jnp.arange(HAD, dtype=jnp.int32)[None, :]
    parity = jnp.zeros((HAD, HAD), jnp.int32)
    for bit in range(HAD.bit_length() - 1):
        parity = parity + jnp.bitwise_and(jnp.right_shift(row_index, bit), 1) * jnp.bitwise_and(
            jnp.right_shift(col_index, bit), 1
        )
    return jnp.where(parity % 2 == 0, 1.0, -1.0).astype(jnp.bfloat16)


def rotate_blocks(hidden, sign_bits):
    signs = (2 * sign_bits - 1).astype(jnp.bfloat16)
    signed = hidden * signs[None, :]
    blocks = signed.reshape(hidden.shape[0] * (hidden.shape[1] // HAD), HAD)
    turned = jnp.dot(blocks, hadamard(), preferred_element_type=jnp.float32) * HAD ** (-0.5)
    return turned.reshape(hidden.shape).astype(jnp.bfloat16)


def local(tokens, gate_weight, up_weight, down_weight, sign_bits):
    values = tokens.astype(jnp.float32)
    local_squares = jnp.sum(values * values, axis=1)
    row_squares = lax.psum(local_squares, "gx")
    inverse = lax.rsqrt(row_squares / D + epsilon)
    normed = (values * inverse[:, None]).astype(jnp.bfloat16)
    gathered = lax.all_gather(normed, "gy", axis=0, tiled=True)
    units = gate_weight.shape[1]
    rows = gathered
    gate_part = jnp.dot(rows, gate_weight, preferred_element_type=jnp.float32)
    up_part = jnp.dot(rows, up_weight, preferred_element_type=jnp.float32)
    summed = lax.psum_scatter(
        jnp.concatenate([gate_part, up_part], axis=1).astype(jnp.bfloat16),
        "gx",
        scatter_dimension=0,
        tiled=True,
    ).astype(jnp.float32)
    hidden = (jax.nn.silu(summed[:, :units]) * summed[:, units:]).astype(jnp.bfloat16)
    rotated = rotate_blocks(hidden, sign_bits)
    full_rows = lax.all_gather(rotated, "gx", axis=0, tiled=True)
    rows = full_rows
    return lax.psum_scatter(
        jnp.dot(rows, down_weight, preferred_element_type=jnp.float32).astype(jnp.bfloat16),
        "gy",
        scatter_dimension=0,
        tiled=True,
    )


def solution(mesh):
    return jax.shard_map(
        local,
        mesh=mesh,
        in_specs=(P("gy", "gx"), P("gx", "gy"), P("gx", "gy"), P("gy", "gx"), P("gy")),
        out_specs=P("gy", "gx"),
        check_vma=False,
    )
```

profile of v0, /device:TPU:1, one launch (start us, length us, event | category | flops | bytes accessed | tf_op | source)
XLA Modules:
  0.0 1010.2 jit_solution(14493499187882644353)
XLA Ops:
  6.5 0.0 copy-start
  6.5 0.0 reduce-scatter.3.cloned.1.call-start
  6.5 1.0 fusion.2
  7.5 70.6 %psum.7 = f32[32]{0:T(128)S(1)} all-reduce(f32[32]{0:T(128)S(1)} %fusion.2), channel_id=1, replica_groups=mesh['gx'=32,'gy'=16] {'gx'}, use_global_device_ids=true, to_apply=%region_1.0 | all-reduce | flops 32 | bytes 256 | tf_op jit(solution)/shard_map/psum | solution.py:35
  78.1 0.8 fusion.3
  78.9 36.0 %all_gather.6 = bf16[512,512]{1,0:T(8,128)(2,1)S(1)} all-gather(bf16[32,512]{1,0:T(8,128)(2,1)S(1)} %fusion.3), channel_id=1, replica_groups=mesh['gx'=32,'gy'=16] {'gy'}, dimensions={0}, use_global_device_ids=true | all-gather | bytes 557056 | tf_op jit(solution)/shard_map/all_gather | solution.py:38
  114.9 1.1 convolution_convert_fusion
  116.1 0.3 copy-done.2
  116.4 1.1 convolution_convert_fusion.1
  117.5 2.0 pad_maximum_fusion
  119.5 0.0 reduce-scatter.3.cloned.1.call-update
  119.5 0.0 all-gather.2.cloned.1.call-start
  119.6 0.6 copy-done.1
  120.2 660.9 %reduce-scatter.3.cloned.1.call-done = bf16[16,3328]{1,0:T(8,128)(2,1)} async-done(((bf16[512,3328]{1,0:T(8,128)(2,1)}), bf16[16,3328]{1,0:T(8,128)(2,1)}) %reduce-scatter.3.cloned.1.call-update) | async-done | bytes 106512 | tf_op jit(solution)/shard_map/reduce_scatter | solution.py:43
  781.1 0.9 convert_element_type.30
  782.1 0.1 reshape.105
  782.1 0.3 fusion
  782.5 0.7 convert_element_type.35
  783.2 0.0 all-gather.2.cloned.1.call-update
  783.2 0.0 reduce-scatter.5.cloned.1.call-start
  783.3 147.5 %all-gather.2.cloned.1.call-done = bf16[512,1664]{1,0:T(8,128)(2,1)} async-done(((bf16[16,1664]{1,0:T(8,128)(2,1)}), bf16[512,1664]{1,0:T(8,128)(2,1)}) %all-gather.2.cloned.1.call-update) | async-done | bytes 1703952 | tf_op jit(solution)/shard_map/all_gather | solution.py:51
  930.8 3.4 convolution_convert_fusion.2
  934.2 0.0 reduce-scatter.5.cloned.1.call-update
  934.2 69.5 %reduce-scatter.5.cloned.1.call-done = bf16[32,512]{1,0:T(8,128)(2,1)} async-done(((bf16[512,512]{1,0:T(8,128)(2,1)}), bf16[32,512]{1,0:T(8,128)(2,1)}) %reduce-scatter.5.cloned.1.call-update) | async-done | bytes 32784 | tf_op jit(solution)/shard_map/reduce_scatter | solution.py:53
  (12 shorter events, 0.1 us)
Async XLA Ops:
  6.5 108.4 %copy-start = (bf16[512,1664]{1,0:T(8,128)(2,1)S(1)}, bf16[512,1664]{1,0:T(8,128)(2,1)}, u32[]{:S(2)}) copy-start(bf16[512,1664]{1,0:T(8,128)(2,1)} %param.7) | copy-start | bytes 5111812
  6.5 774.5 %reduce-scatter.3.cloned.1.call-start = ((), (), s32[]{:S(2)}) async-start(), calls=%async_computation.2 | async-start | bytes 3514368 | tf_op jit(solution)/shard_map/reduce_scatter | solution.py:43
  114.9 1.5 copy-start.2
  119.5 0.7 copy-start.1
  119.5 811.4 %copy-start.3 = (bf16[1664,512]{1,0:T(8,128)(2,1)S(1)}, bf16[1664,512]{1,0:T(8,128)(2,1)}, u32[]{:S(2)}) copy-start(bf16[1664,512]{1,0:T(8,128)(2,1)} %param.8) | copy-start | bytes 5111812
  119.5 811.3 %all-gather.2.cloned.1.call-start = ((), (), s32[]{:S(2)}) async-start(), calls=%async_computation.3 | async-start | bytes 1757184 | tf_op jit(solution)/shard_map/all_gather | solution.py:51
  783.2 220.5 %reduce-scatter.5.cloned.1.call-start = ((), (), s32[]{:S(2)}) async-start(), calls=%async_computation.4 | async-start | bytes 557056 | tf_op jit(solution)/shard_map/reduce_scatter | solution.py:53
Sparse Core Ops, SparseCore 0:
  119.6 661.4 reduce-scatter.2
  784.7 146.0 all-gather.1
  934.3 69.3 reduce-scatter.4
where the time goes:
time: 1010 us
  waiting for transfers between devices  878 us (87%)
  blocking collectives  107 us (11%)
  between operations  13.2 us (1%)
    reduce_scatter x1, waiting for transfers between devices, local(): lax.psum_scatter(jnp.concatenate([gate_part, up_part], axis=1).astype(jnp...  661 us
    all_gather x1, waiting for transfers between devices, local(): full_rows = lax.all_gather(rotated, 'gx', axis=0, tiled=True)  148 us
    psum x1, blocking collectives, local(): row_squares = lax.psum(local_squares, 'gx')  70.6 us
    reduce_scatter x1, waiting for transfers between devices, local(): lax.psum_scatter(jnp.dot(rows, down_weight, preferred_element_type=jnp.fl...  69.5 us
    all_gather x1, blocking collectives, local(): gathered = lax.all_gather(normed, 'gy', axis=0, tiled=True)  36 us
  transfers between devices with their start and end apart: 3, of which 3 were waited for; matrix products, arithmetic and copies ran while one was open for 0% of the time, Pallas kernels for 0%

commit v1 on v0

v1 whole, which is shorter than its diff:
```python
import jax
import jax.numpy as jnp
import numpy as np
from jax import lax
from jax.experimental import pallas as pl
from jax.experimental.pallas import tpu as pltpu
from jax.sharding import Mesh, PartitionSpec as P

D = 16384
HAD = 128
UNITS = 1664
LANES = 128
EPSILON = 1e-05

AXES = ("zh", "zl", "xh", "y", "xl", "c")
SIZES = (4, 4, 2, 4, 2, 2)
GX = ("zh", "zl", "xh")
GY = ("y", "xl", "c")
Z = ("zh", "zl")
f32, bf16 = jnp.float32, jnp.bfloat16


def along_z(x, d):
    return lax.ppermute(x, Z, [(i, (i + d) % 16) for i in range(16)])


def across_x(x):
    return lax.ppermute(x, "xh", [(0, 1), (1, 0)])


def dot(a, b):
    return jnp.dot(a, b, preferred_element_type=f32)


def hadamard():
    i = np.arange(HAD)
    both = i[:, None] & i[None, :]
    parity = np.zeros_like(both)
    for bit in range(7):
        parity ^= (both >> bit) & 1
    return jnp.asarray(1.0 - 2.0 * parity, bf16)


def finish(own, a, b, c, signs, had, out):
    def total(lo, hi):
        return (own[:, lo:hi].astype(f32) + a[:, lo:hi].astype(f32)
                + b[:, lo:hi].astype(f32) + c[:, lo:hi].astype(f32))

    squares = jnp.sum(total(2 * UNITS, 2 * UNITS + LANES), axis=1, keepdims=True)
    inverse = lax.rsqrt(squares / D + EPSILON)
    for k in range(UNITS // HAD):
        lo = k * HAD
        gate = total(lo, lo + HAD) * inverse
        up = total(UNITS + lo, UNITS + lo + HAD) * inverse
        hidden = (gate / (1.0 + jnp.exp(-gate)) * up).astype(bf16)
        signed = hidden * signs[:, lo:lo + HAD]
        out[:, lo:lo + HAD] = (dot(signed, had[...]) * HAD ** (-0.5)).astype(bf16)


def local(tokens, gate_weight, up_weight, down_weight, sign_bits):
    zh, zl, xh = lax.axis_index("zh"), lax.axis_index("zl"), lax.axis_index("xh")

    sent = jnp.concatenate([tokens] * 8, axis=0)
    some = lax.all_to_all(sent, ("y", "xl"), 0, 0, tiled=True)
    gathered = lax.all_gather(some, "c", axis=0, tiled=True)

    rows = gathered.reshape(2, 4, 64, 512)

    def gate_of(x):
        t = lax.dynamic_index_in_dim(rows, x, 0, keepdims=False).reshape(256, 512)
        return dot(t, gate_weight)

    def up_of(d):
        t = lax.dynamic_index_in_dim(rows, (zl + d) % 4, 1, keepdims=False).reshape(128, 512)
        v = t.astype(f32)
        v = v * v
        squares = v[:, :128] + v[:, 128:256] + v[:, 256:384] + v[:, 384:]
        return jnp.concatenate([dot(t, up_weight).astype(bf16), squares.astype(bf16)], axis=1)

    gate_in = across_x(gate_of(1 - xh).astype(bf16))
    up2 = up_of(2).reshape(2, 64, UNITS + LANES)
    up_a = along_z(up2[:, :32], 2)
    up_b = along_z(up2[:, 32:], -2)
    up_c = along_z(up_of(1), 1)
    up_d = along_z(up_of(3), -1)
    up_own = up_of(0).astype(f32).reshape(2, 64, UNITS + LANES)
    gate_own = gate_of(xh)

    gate = (gate_own + gate_in.astype(f32)).astype(bf16).reshape(4, 64, UNITS)

    def gate_class(d):
        return lax.dynamic_index_in_dim(gate, (zl + d) % 4, 0, keepdims=False)

    gate2 = gate_class(2)
    gate_a = along_z(gate2[:32], 2)
    gate_b = along_z(gate2[32:], -2)
    gate_c = along_z(gate_class(1), 1)
    gate_d = along_z(gate_class(3), -1)
    up = up_own + up_c.reshape(up_own.shape).astype(f32) + up_d.reshape(up_own.shape).astype(f32)
    up = up + jnp.concatenate([up_a, up_b], axis=1).astype(f32)
    up_in = across_x(lax.dynamic_index_in_dim(up, 1 - xh, 0, keepdims=False).astype(bf16))
    up = lax.dynamic_index_in_dim(up, xh, 0, keepdims=False) + up_in.astype(f32)
    gate = gate_class(0).astype(f32) + gate_c.astype(f32) + gate_d.astype(f32)
    gate = gate + jnp.concatenate([gate_a, gate_b], axis=0).astype(f32)

    both = jnp.concatenate([gate.astype(bf16), up.astype(bf16)], axis=1).reshape(2, 4, 8, 2 * UNITS + LANES)

    def both_class(d):
        return lax.dynamic_index_in_dim(both, (zh + d) % 4, 1, keepdims=False).reshape(16, 2 * UNITS + LANES)

    far_c = along_z(both_class(2), 8)
    far_a = along_z(both_class(1), 4)
    far_b = along_z(both_class(3), -4)

    signs = (2 * sign_bits - 1).astype(bf16).reshape(1, UNITS)
    rotated = pl.pallas_call(
        finish,
        out_shape=jax.ShapeDtypeStruct((16, UNITS), bf16),
    )(both_class(0), far_a, far_b, far_c, signs, hadamard())

    from_p2 = along_z(rotated, 8)
    from_m1 = along_z(rotated, 4)
    from_p1 = along_z(rotated, -4)
    far = jnp.concatenate([rotated, from_p1, from_p2, from_m1], axis=0)
    near = lax.all_gather(far, "xh", axis=0, tiled=True)
    n2a = along_z(near[:64], 2)
    n2b = along_z(near[64:], -2)
    n3 = along_z(near, 1)
    n1 = along_z(near, -1)
    pieces = [dot(v, down_weight).astype(bf16) for v in (near, n1, n2a, n2b, n3)]
    out = jnp.concatenate(pieces, axis=0)

    r = lax.broadcasted_iota(jnp.int32, (512, 512), 1)
    d, x, j, half, k = r // 128, r // 64 % 2, r // 16 % 4, r // 8 % 2, r % 8
    shift = jnp.where(d == 0, 0, jnp.where(d == 1, 1, jnp.where(d == 3, -1, jnp.where(x == 0, -2, 2))))
    sender = (zh * 4 + zl + shift + 16) % 16
    place = (((x * 4 + sender % 4) * 2 + half) * 4 + (sender // 4 + j) % 4) * 8 + k
    order = (place == lax.broadcasted_iota(jnp.int32, (512, 512), 0)).astype(bf16)
    out = dot(order, out).astype(bf16)

    parts = lax.all_to_all(out.reshape(16, 32, 512), ("c", "y", "xl"), 0, 0, tiled=True)
    return jnp.sum(parts.astype(f32), axis=0).astype(bf16)


def solution(mesh):
    fine = Mesh(mesh.devices.reshape(SIZES), AXES)
    return jax.shard_map(
        local,
        mesh=fine,
        in_specs=(P(GY, GX), P(GX, GY), P(GX, GY), P(GY, GX), P(GY)),
        out_specs=P(GY, GX),
        check_vma=False,
    )
```

time: 1010 us -> 193 us (0.19)
  the two profiles are of different devices: /device:TPU:1 before, /device:TPU:39 now
where the time goes in v1:
time: 193 us; the launch traced here: 192 us
  starting transfers between devices  88.9 us (46%)
  waiting for transfers between devices  49.5 us (26%)
  blocking collectives  33.3 us (17%)
  local copies, waits for them, and re-layouts  9.19 us (5%)
  matrix products  5.72 us (3%)
  other arithmetic  2.98 us (2%)
  Pallas kernels  2 us (1%)
    ppermute x18, starting transfers between devices, along_z(): return lax.ppermute(x, Z, [(i, (i + d) % 16) for i in range(16)])  76.6 us
    ppermute x18, waiting for transfers between devices, along_z(): return lax.ppermute(x, Z, [(i, (i + d) % 16) for i in range(16)])  45.4 us
    all_to_all x1, blocking collectives, local(): lax.all_to_all(out.reshape(16, 32, 512), ('c', 'y', 'xl'), 0, 0, tiled=True)  22.4 us
    ppermute x2, starting transfers between devices, across_x(): return lax.ppermute(x, 'xh', [(0, 1), (1, 0)])  6.92 us
    unnamed x21, local copies, waits for them, and re-layouts  6.88 us
    all_gather x1, blocking collectives, local(): near = lax.all_gather(far, 'xh', axis=0, tiled=True)  6.88 us
    dot_general x12, matrix products, dot(): return jnp.dot(a, b, preferred_element_type=f32)  5.72 us
    all_to_all x1, starting transfers between devices, local(): some = lax.all_to_all(sent, ('y', 'xl'), 0, 0, tiled=True)  5.37 us
  transfers between devices with their start and end apart: 21, of which 10 were waited for; matrix products, arithmetic and copies ran while one was open for 3% of the time, Pallas kernels for 0%

profile of v1, /device:TPU:39, one launch (start us, length us, event | category | flops | bytes accessed | tf_op | source)
XLA Modules:
  0.0 192.1 jit_solution(3951552671102764994)
XLA Ops:
  7.0 5.4 %all-to-all-start = ((bf16[8,32,512]{2,1,0:T(8,128)(2,1)}), bf16[8,32,512]{2,1,0:T(8,128)(2,1)}, u32[]{:S(2)}, u32[]{:S(2)}) async-start(bf16[8,32,512]{2,1,0:T(8,128)(2,1)} %bitcast.88), calls=%async_computation | async-start | bytes 524288 | tf_op jit(solution)/shard_map/all_to_all | solution.py:64
  13.7 4.0 %all-to-all-done = bf16[8,32,512]{2,1,0:T(8,128)(2,1)} async-done(((bf16[8,32,512]{2,1,0:T(8,128)(2,1)}), bf16[8,32,512]{2,1,0:T(8,128)(2,1)}, u32[]{:S(2)}, u32[]{:S(2)}) %all-to-all-start) | async-done | bytes 262176 | tf_op jit(solution)/shard_map/all_to_all | solution.py:64
  17.7 4.1 %all_gather.6 = bf16[512,512]{1,0:T(8,128)(2,1)S(1)} all-gather(bf16[256,512]{1,0:T(8,128)(2,1)} %bitcast.1), channel_id=1, replica_groups=mesh['zh'=4,'zl'=4,'xh'=2,'y'=4,'xl'=2,'c'=2] {'c'}, dimensions={0}, use_global_device_ids=true | all-gather | bytes 786432 | tf_op jit(solution)/shard_map/all_gather | solution.py:65
  22.5 3.2 %collective-permute-start = (bf16[256,1664]{1,0:T(8,128)(2,1)S(1)}, bf16[256,1664]{1,0:T(8,128)(2,1)S(1)}, u32[]{:S(2)}, u32[]{:S(2)}) collective-permute-start(bf16[256,1664]{1,0:T(8,128)(2,1)S(1)} %convolution_convert_fusion), channel_id=1, source_target_pairs={{0,16},{16,0},{1,17},{17,1},{2,18},{18,2},{3,19},{19,3},{4,20},{20... | collective-permute-start | bytes 2555912 | tf_op jit(solution)/shard_map/ppermute | solution.py:28
  26.4 4.9 %collective-permute-start.7 = (bf16[2,32,1792]{2,1,0:T(8,128)(2,1)S(1)}, bf16[2,32,1792]{2,1,0:T(8,128)(2,1)S(1)}, u32[]{:S(2)}, u32[]{:S(2)}) collective-permute-start(bf16[2,32,1792]{2,1,0:T(8,128)(2,1)S(1)} %get-tuple-element.15), channel_id=1, source_target_pairs={{0,64},{32,96},{64,128},{96,160},{128,192},{160,224},{192,256},{22... | collective-permute-start | bytes 688136 | tf_op jit(solution)/shard_map/ppermute | solution.py:24
  31.3 7.7 %collective-permute-start.8 = (bf16[2,32,1792]{2,1,0:T(8,128)(2,1)S(1)}, bf16[2,32,1792]{2,1,0:T(8,128)(2,1)S(1)}, u32[]{:S(2)}, u32[]{:S(2)}) collective-permute-start(bf16[2,32,1792]{2,1,0:T(8,128)(2,1)S(1)} %get-tuple-element.16), channel_id=1, source_target_pairs={{0,448},{32,480},{64,0},{96,32},{128,64},{160,96},{192,128},{224,1... | collective-permute-start | bytes 688136 | tf_op jit(solution)/shard_map/ppermute | solution.py:24
  42.0 3.4 %collective-permute-start.6 = (bf16[128,1792]{1,0:T(8,128)(2,1)S(1)}, bf16[128,1792]{1,0:T(8,128)(2,1)S(1)}, u32[]{:S(2)}, u32[]{:S(2)}) collective-permute-start(bf16[128,1792]{1,0:T(8,128)(2,1)S(1)} %pad_maximum_fusion.1), channel_id=1, source_target_pairs={{0,480},{32,0},{64,32},{96,64},{128,96},{160,128},{192,160},{224,1... | collective-permute-start | bytes 1376264 | tf_op jit(solution)/shard_map/ppermute | solution.py:24
  47.7 8.2 %collective-permute-done.5 = bf16[128,1792]{1,0:T(8,128)(2,1)S(1)} collective-permute-done((bf16[128,1792]{1,0:T(8,128)(2,1)S(1)}, bf16[128,1792]{1,0:T(8,128)(2,1)S(1)}, u32[]{:S(2)}, u32[]{:S(2)}) %collective-permute-start.5) | collective-permute-done | bytes 458784 | tf_op jit(solution)/shard_map/ppermute | solution.py:24
  57.7 3.8 %collective-permute-start.9 = (bf16[64,1792]{1,0:T(8,128)(2,1)S(1)}, bf16[64,1792]{1,0:T(8,128)(2,1)S(1)}, u32[]{:S(2)}, u32[]{:S(2)}) collective-permute-start(bf16[64,1792]{1,0:T(8,128)(2,1)S(1)} %fusion.53), channel_id=1, source_target_pairs={{0,16},{16,0},{1,17},{17,1},{2,18},{18,2},{3,19},{19,3},{4,20},{20... | collective-permute-start | bytes 688136 | tf_op jit(solution)/shard_map/ppermute | solution.py:28
  64.1 4.1 %collective-permute-start.2 = (bf16[64,1664]{1,0:T(8,128)(2,1)S(1)}, bf16[64,1664]{1,0:T(8,128)(2,1)S(1)}, u32[]{:S(2)}, u32[]{:S(2)}) collective-permute-start(bf16[64,1664]{1,0:T(8,128)(2,1)S(1)} %get-tuple-element.8), channel_id=1, source_target_pairs={{0,480},{32,0},{64,32},{96,64},{128,96},{160,128},{192,160},{224,1... | collective-permute-start | bytes 638984 | tf_op jit(solution)/shard_map/ppermute | solution.py:24
  68.2 4.9 %collective-permute-start.3 = (bf16[32,1664]{1,0:T(8,128)(2,1)S(1)}, bf16[32,1664]{1,0:T(8,128)(2,1)S(1)}, u32[]{:S(2)}, u32[]{:S(2)}) collective-permute-start(bf16[32,1664]{1,0:T(8,128)(2,1)S(1)} %get-tuple-element.5), channel_id=1, source_target_pairs={{0,64},{32,96},{64,128},{96,160},{128,192},{160,224},{192,256},{22... | collective-permute-start | bytes 319496 | tf_op jit(solution)/shard_map/ppermute | solution.py:24
  73.1 3.0 %collective-permute-start.4 = (bf16[32,1664]{1,0:T(8,128)(2,1)S(1)}, bf16[32,1664]{1,0:T(8,128)(2,1)S(1)}, u32[]{:S(2)}, u32[]{:S(2)}) collective-permute-start(bf16[32,1664]{1,0:T(8,128)(2,1)S(1)} %get-tuple-element.6), channel_id=1, source_target_pairs={{0,448},{32,480},{64,0},{96,32},{128,64},{160,96},{192,128},{224,1... | collective-permute-start | bytes 319496 | tf_op jit(solution)/shard_map/ppermute | solution.py:24
  76.3 3.6 %collective-permute-done.4 = bf16[32,1664]{1,0:T(8,128)(2,1)S(1)} collective-permute-done((bf16[32,1664]{1,0:T(8,128)(2,1)S(1)}, bf16[32,1664]{1,0:T(8,128)(2,1)S(1)}, u32[]{:S(2)}, u32[]{:S(2)}) %collective-permute-start.4) | collective-permute-done | bytes 106528 | tf_op jit(solution)/shard_map/ppermute | solution.py:24
  80.7 7.2 %collective-permute-start.10 = (bf16[16,3456]{1,0:T(8,128)(2,1)S(1)}, bf16[16,3456]{1,0:T(8,128)(2,1)S(1)}, u32[]{:S(2)}, u32[]{:S(2)}) collective-permute-start(bf16[16,3456]{1,0:T(8,128)(2,1)S(1)} %get-tuple-element.19), channel_id=1, source_target_pairs={{0,128},{32,160},{64,192},{96,224},{128,256},{160,288},{192,320},{... | collective-permute-start | bytes 331784 | tf_op jit(solution)/shard_map/ppermute | solution.py:24
  89.9 9.0 %collective-permute-start.12 = (bf16[16,3456]{1,0:T(8,128)(2,1)S(1)}, bf16[16,3456]{1,0:T(8,128)(2,1)S(1)}, u32[]{:S(2)}, u32[]{:S(2)}) collective-permute-start(bf16[16,3456]{1,0:T(8,128)(2,1)S(1)} %get-tuple-element.17), channel_id=1, source_target_pairs={{0,256},{32,288},{64,320},{96,352},{128,384},{160,416},{192,448},{... | collective-permute-start | bytes 331784 | tf_op jit(solution)/shard_map/ppermute | solution.py:24
  99.0 17.7 %collective-permute-done.12.c = bf16[16,3456]{1,0:T(8,128)(2,1)S(1)} collective-permute-done((bf16[16,3456]{1,0:T(8,128)(2,1)S(1)}, bf16[16,3456]{1,0:T(8,128)(2,1)S(1)}, u32[]{:S(2)}, u32[]{:S(2)}) %collective-permute-start.12) | collective-permute-done | bytes 110624 | tf_op jit(solution)/shard_map/ppermute | solution.py:24
  121.3 4.8 %collective-permute-start.14 = (bf16[16,1664]{1,0:T(8,128)(2,1)}, bf16[16,1664]{1,0:T(8,128)(2,1)S(1)}, u32[]{:S(2)}, u32[]{:S(2)}) collective-permute-start(bf16[16,1664]{1,0:T(8,128)(2,1)} %shard_map.64), channel_id=1, source_target_pairs={{0,256},{32,288},{64,320},{96,352},{128,384},{160,416},{192,448},{... | collective-permute-start | bytes 159752 | tf_op jit(solution)/shard_map/ppermute | solution.py:24
  126.1 7.3 %collective-permute-start.15 = (bf16[16,1664]{1,0:T(8,128)(2,1)}, bf16[16,1664]{1,0:T(8,128)(2,1)S(1)}, u32[]{:S(2)}, u32[]{:S(2)}) collective-permute-start(bf16[16,1664]{1,0:T(8,128)(2,1)} %shard_map.64), channel_id=1, source_target_pairs={{0,128},{32,160},{64,192},{96,224},{128,256},{160,288},{192,320},{... | collective-permute-start | bytes 159752 | tf_op jit(solution)/shard_map/ppermute | solution.py:24
  135.3 3.5 %collective-permute-done.15 = bf16[16,1664]{1,0:T(8,128)(2,1)S(1)} collective-permute-done((bf16[16,1664]{1,0:T(8,128)(2,1)}, bf16[16,1664]{1,0:T(8,128)(2,1)S(1)}, u32[]{:S(2)}, u32[]{:S(2)}) %collective-permute-start.15) | collective-permute-done | bytes 53280 | tf_op jit(solution)/shard_map/ppermute | solution.py:24
  139.6 6.9 %all_gather.7 = bf16[128,1664]{1,0:T(8,128)(2,1)S(1)} all-gather(bf16[64,1664]{1,0:T(8,128)(2,1)S(1)} %pad_maximum_fusion.4), channel_id=1, replica_groups=mesh['zh'=4,'zl'=4,'xh'=2,'y'=4,'xl'=2,'c'=2] {'xh'}, dimensions={0}, use_global_device_ids=true | all-gather | bytes 638976 | tf_op jit(solution)/shard_map/all_gather | solution.py:125
  148.4 3.4 %collective-permute-start.19 = (bf16[128,1664]{1,0:T(8,128)(2,1)S(1)}, bf16[128,1664]{1,0:T(8,128)(2,1)S(1)}, u32[]{:S(2)}, u32[]{:S(2)}) collective-permute-start(bf16[128,1664]{1,0:T(8,128)(2,1)S(1)} %all_gather.7), channel_id=1, source_target_pairs={{0,32},{32,64},{64,96},{96,128},{128,160},{160,192},{192,224},{224... | collective-permute-start | bytes 1277960 | tf_op jit(solution)/shard_map/ppermute | solution.py:24
  153.7 5.5 %collective-permute-start.18 = (bf16[64,1664]{1,0:T(8,128)(2,1)S(1)}, bf16[64,1664]{1,0:T(8,128)(2,1)S(1)}, u32[]{:S(2)}, u32[]{:S(2)}) collective-permute-start(bf16[64,1664]{1,0:T(8,128)(2,1)S(1)} %get-tuple-element.21), channel_id=1, source_target_pairs={{0,448},{32,480},{64,0},{96,32},{128,64},{160,96},{192,128},{224,1... | collective-permute-start | bytes 638984 | tf_op jit(solution)/shard_map/ppermute | solution.py:24
  160.0 7.0 %collective-permute-done.17 = bf16[64,1664]{1,0:T(8,128)(2,1)S(1)} collective-permute-done((bf16[64,1664]{1,0:T(8,128)(2,1)S(1)}, bf16[64,1664]{1,0:T(8,128)(2,1)S(1)}, u32[]{:S(2)}, u32[]{:S(2)}) %collective-permute-start.17) | collective-permute-done | bytes 213024 | tf_op jit(solution)/shard_map/ppermute | solution.py:24
  169.1 22.4 %all_to_all.17 = bf16[16,32,512]{2,1,0:T(8,128)(2,1)S(1)} all-to-all(bf16[16,32,512]{2,1,0:T(8,128)(2,1)S(1)} %bitcast.85), channel_id=1, replica_groups=mesh['zh'=4,'zl'=4,'xh'=2,'y'=4,'xl'=2,'c'=2] {'c','y','xl'}, dimensions={0} | all-to-all | bytes 1048576 | tf_op jit(solution)/shard_map/all_to_all | solution.py:141
  (89 shorter events, 37.0 us)
Async XLA Ops:
  0.0 159.2 %copy-start = (bf16[1664,512]{1,0:T(8,128)(2,1)S(1)}, bf16[1664,512]{1,0:T(8,128)(2,1)}, u32[]{:S(2)}) copy-start(bf16[1664,512]{1,0:T(8,128)(2,1)} %param.9) | copy-start | bytes 5111812
  0.0 21.9 %copy-start.2 = (bf16[512,1664]{1,0:T(8,128)(2,1)S(1)}, bf16[512,1664]{1,0:T(8,128)(2,1)}, u32[]{:S(2)}) copy-start(bf16[512,1664]{1,0:T(8,128)(2,1)} %param.7) | copy-start | bytes 5111812
  7.0 10.8 %all-to-all-start = ((bf16[8,32,512]{2,1,0:T(8,128)(2,1)}), bf16[8,32,512]{2,1,0:T(8,128)(2,1)}, u32[]{:S(2)}, u32[]{:S(2)}) async-start(bf16[8,32,512]{2,1,0:T(8,128)(2,1)} %bitcast.88), calls=%async_computation | async-start | bytes 524288 | tf_op jit(solution)/shard_map/all_to_all | solution.py:64
  22.5 38.9 %collective-permute-start = (bf16[256,1664]{1,0:T(8,128)(2,1)S(1)}, bf16[256,1664]{1,0:T(8,128)(2,1)S(1)}, u32[]{:S(2)}, u32[]{:S(2)}) collective-permute-start(bf16[256,1664]{1,0:T(8,128)(2,1)S(1)} %convolution_convert_fusion), channel_id=1, source_target_pairs={{0,16},{16,0},{1,17},{17,1},{2,18},{18,2},{3,19},{19,3},{4,20},{20... | collective-permute-start | bytes 2555912 | tf_op jit(solution)/shard_map/ppermute | solution.py:28
  26.4 21.3 %collective-permute-start.7 = (bf16[2,32,1792]{2,1,0:T(8,128)(2,1)S(1)}, bf16[2,32,1792]{2,1,0:T(8,128)(2,1)S(1)}, u32[]{:S(2)}, u32[]{:S(2)}) collective-permute-start(bf16[2,32,1792]{2,1,0:T(8,128)(2,1)S(1)} %get-tuple-element.15), channel_id=1, source_target_pairs={{0,64},{32,96},{64,128},{96,160},{128,192},{160,224},{192,256},{22... | collective-permute-start | bytes 688136 | tf_op jit(solution)/shard_map/ppermute | solution.py:24
  31.3 16.4 %collective-permute-start.8 = (bf16[2,32,1792]{2,1,0:T(8,128)(2,1)S(1)}, bf16[2,32,1792]{2,1,0:T(8,128)(2,1)S(1)}, u32[]{:S(2)}, u32[]{:S(2)}) collective-permute-start(bf16[2,32,1792]{2,1,0:T(8,128)(2,1)S(1)} %get-tuple-element.16), channel_id=1, source_target_pairs={{0,448},{32,480},{64,0},{96,32},{128,64},{160,96},{192,128},{224,1... | collective-permute-start | bytes 688136 | tf_op jit(solution)/shard_map/ppermute | solution.py:24
  39.5 16.3 %collective-permute-start.5 = (bf16[128,1792]{1,0:T(8,128)(2,1)S(1)}, bf16[128,1792]{1,0:T(8,128)(2,1)S(1)}, u32[]{:S(2)}, u32[]{:S(2)}) collective-permute-start(bf16[128,1792]{1,0:T(8,128)(2,1)S(1)} %pad_maximum_fusion), channel_id=1, source_target_pairs={{0,32},{32,64},{64,96},{96,128},{128,160},{160,192},{192,224},{224... | collective-permute-start | bytes 1376264 | tf_op jit(solution)/shard_map/ppermute | solution.py:24
  42.0 15.4 %collective-permute-start.6 = (bf16[128,1792]{1,0:T(8,128)(2,1)S(1)}, bf16[128,1792]{1,0:T(8,128)(2,1)S(1)}, u32[]{:S(2)}, u32[]{:S(2)}) collective-permute-start(bf16[128,1792]{1,0:T(8,128)(2,1)S(1)} %pad_maximum_fusion.1), channel_id=1, source_target_pairs={{0,480},{32,0},{64,32},{96,64},{128,96},{160,128},{192,160},{224,1... | collective-permute-start | bytes 1376264 | tf_op jit(solution)/shard_map/ppermute | solution.py:24
  57.7 18.4 %collective-permute-start.9 = (bf16[64,1792]{1,0:T(8,128)(2,1)S(1)}, bf16[64,1792]{1,0:T(8,128)(2,1)S(1)}, u32[]{:S(2)}, u32[]{:S(2)}) collective-permute-start(bf16[64,1792]{1,0:T(8,128)(2,1)S(1)} %fusion.53), channel_id=1, source_target_pairs={{0,16},{16,0},{1,17},{17,1},{2,18},{18,2},{3,19},{19,3},{4,20},{20... | collective-permute-start | bytes 688136 | tf_op jit(solution)/shard_map/ppermute | solution.py:28
  62.1 17.7 %collective-permute-start.1 = (bf16[64,1664]{1,0:T(8,128)(2,1)S(1)}, bf16[64,1664]{1,0:T(8,128)(2,1)S(1)}, u32[]{:S(2)}, u32[]{:S(2)}) collective-permute-start(bf16[64,1664]{1,0:T(8,128)(2,1)S(1)} %get-tuple-element.7), channel_id=1, source_target_pairs={{0,32},{32,64},{64,96},{96,128},{128,160},{160,192},{192,224},{224... | collective-permute-start | bytes 638984 | tf_op jit(solution)/shard_map/ppermute | solution.py:24
  64.1 15.8 %collective-permute-start.2 = (bf16[64,1664]{1,0:T(8,128)(2,1)S(1)}, bf16[64,1664]{1,0:T(8,128)(2,1)S(1)}, u32[]{:S(2)}, u32[]{:S(2)}) collective-permute-start(bf16[64,1664]{1,0:T(8,128)(2,1)S(1)} %get-tuple-element.8), channel_id=1, source_target_pairs={{0,480},{32,0},{64,32},{96,64},{128,96},{160,128},{192,160},{224,1... | collective-permute-start | bytes 638984 | tf_op jit(solution)/shard_map/ppermute | solution.py:24
  68.2 8.1 %collective-permute-start.3 = (bf16[32,1664]{1,0:T(8,128)(2,1)S(1)}, bf16[32,1664]{1,0:T(8,128)(2,1)S(1)}, u32[]{:S(2)}, u32[]{:S(2)}) collective-permute-start(bf16[32,1664]{1,0:T(8,128)(2,1)S(1)} %get-tuple-element.5), channel_id=1, source_target_pairs={{0,64},{32,96},{64,128},{96,160},{128,192},{160,224},{192,256},{22... | collective-permute-start | bytes 319496 | tf_op jit(solution)/shard_map/ppermute | solution.py:24
  73.1 6.7 %collective-permute-start.4 = (bf16[32,1664]{1,0:T(8,128)(2,1)S(1)}, bf16[32,1664]{1,0:T(8,128)(2,1)S(1)}, u32[]{:S(2)}, u32[]{:S(2)}) collective-permute-start(bf16[32,1664]{1,0:T(8,128)(2,1)S(1)} %get-tuple-element.6), channel_id=1, source_target_pairs={{0,448},{32,480},{64,0},{96,32},{128,64},{160,96},{192,128},{224,1... | collective-permute-start | bytes 319496 | tf_op jit(solution)/shard_map/ppermute | solution.py:24
  80.7 18.2 %collective-permute-start.10 = (bf16[16,3456]{1,0:T(8,128)(2,1)S(1)}, bf16[16,3456]{1,0:T(8,128)(2,1)S(1)}, u32[]{:S(2)}, u32[]{:S(2)}) collective-permute-start(bf16[16,3456]{1,0:T(8,128)(2,1)S(1)} %get-tuple-element.19), channel_id=1, source_target_pairs={{0,128},{32,160},{64,192},{96,224},{128,256},{160,288},{192,320},{... | collective-permute-start | bytes 331784 | tf_op jit(solution)/shard_map/ppermute | solution.py:24
  88.0 11.0 %collective-permute-start.11 = (bf16[16,3456]{1,0:T(8,128)(2,1)S(1)}, bf16[16,3456]{1,0:T(8,128)(2,1)S(1)}, u32[]{:S(2)}, u32[]{:S(2)}) collective-permute-start(bf16[16,3456]{1,0:T(8,128)(2,1)S(1)} %get-tuple-element.18), channel_id=1, source_target_pairs={{0,384},{32,416},{64,448},{96,480},{128,0},{160,32},{192,64},{224,... | collective-permute-start | bytes 331784 | tf_op jit(solution)/shard_map/ppermute | solution.py:24
  89.9 26.7 %collective-permute-start.12 = (bf16[16,3456]{1,0:T(8,128)(2,1)S(1)}, bf16[16,3456]{1,0:T(8,128)(2,1)S(1)}, u32[]{:S(2)}, u32[]{:S(2)}) collective-permute-start(bf16[16,3456]{1,0:T(8,128)(2,1)S(1)} %get-tuple-element.17), channel_id=1, source_target_pairs={{0,256},{32,288},{64,320},{96,352},{128,384},{160,416},{192,448},{... | collective-permute-start | bytes 331784 | tf_op jit(solution)/shard_map/ppermute | solution.py:24
  99.0 17.7 %copy-start.4 = (bf16[16,3456]{1,0:T(8,128)(2,1)}, bf16[16,3456]{1,0:T(8,128)(2,1)S(1)}, u32[]{:S(2)}) copy-start(bf16[16,3456]{1,0:T(8,128)(2,1)S(1)} %collective-permute-done.10.a) | copy-start | bytes 331780
  119.3 14.1 %collective-permute-start.13 = (bf16[16,1664]{1,0:T(8,128)(2,1)}, bf16[16,1664]{1,0:T(8,128)(2,1)S(1)}, u32[]{:S(2)}, u32[]{:S(2)}) collective-permute-start(bf16[16,1664]{1,0:T(8,128)(2,1)} %shard_map.64), channel_id=1, source_target_pairs={{0,384},{32,416},{64,448},{96,480},{128,0},{160,32},{192,64},{224,... | collective-permute-start | bytes 159752 | tf_op jit(solution)/shard_map/ppermute | solution.py:24
  121.3 14.0 %collective-permute-start.14 = (bf16[16,1664]{1,0:T(8,128)(2,1)}, bf16[16,1664]{1,0:T(8,128)(2,1)S(1)}, u32[]{:S(2)}, u32[]{:S(2)}) collective-permute-start(bf16[16,1664]{1,0:T(8,128)(2,1)} %shard_map.64), channel_id=1, source_target_pairs={{0,256},{32,288},{64,320},{96,352},{128,384},{160,416},{192,448},{... | collective-permute-start | bytes 159752 | tf_op jit(solution)/shard_map/ppermute | solution.py:24
  126.1 12.7 %collective-permute-start.15 = (bf16[16,1664]{1,0:T(8,128)(2,1)}, bf16[16,1664]{1,0:T(8,128)(2,1)S(1)}, u32[]{:S(2)}, u32[]{:S(2)}) collective-permute-start(bf16[16,1664]{1,0:T(8,128)(2,1)} %shard_map.64), channel_id=1, source_target_pairs={{0,128},{32,160},{64,192},{96,224},{128,256},{160,288},{192,320},{... | collective-permute-start | bytes 159752 | tf_op jit(solution)/shard_map/ppermute | solution.py:24
  146.4 13.2 %collective-permute-start.16 = (bf16[128,1664]{1,0:T(8,128)(2,1)S(1)}, bf16[128,1664]{1,0:T(8,128)(2,1)S(1)}, u32[]{:S(2)}, u32[]{:S(2)}) collective-permute-start(bf16[128,1664]{1,0:T(8,128)(2,1)S(1)} %all_gather.7), channel_id=1, source_target_pairs={{0,480},{32,0},{64,32},{96,64},{128,96},{160,128},{192,160},{224,1... | collective-permute-start | bytes 1277960 | tf_op jit(solution)/shard_map/ppermute | solution.py:24
  148.4 19.5 %collective-permute-start.19 = (bf16[128,1664]{1,0:T(8,128)(2,1)S(1)}, bf16[128,1664]{1,0:T(8,128)(2,1)S(1)}, u32[]{:S(2)}, u32[]{:S(2)}) collective-permute-start(bf16[128,1664]{1,0:T(8,128)(2,1)S(1)} %all_gather.7), channel_id=1, source_target_pairs={{0,32},{32,64},{64,96},{96,128},{128,160},{160,192},{192,224},{224... | collective-permute-start | bytes 1277960 | tf_op jit(solution)/shard_map/ppermute | solution.py:24
  151.8 15.3 %collective-permute-start.17 = (bf16[64,1664]{1,0:T(8,128)(2,1)S(1)}, bf16[64,1664]{1,0:T(8,128)(2,1)S(1)}, u32[]{:S(2)}, u32[]{:S(2)}) collective-permute-start(bf16[64,1664]{1,0:T(8,128)(2,1)S(1)} %get-tuple-element.22), channel_id=1, source_target_pairs={{0,64},{32,96},{64,128},{96,160},{128,192},{160,224},{192,256},{22... | collective-permute-start | bytes 638984 | tf_op jit(solution)/shard_map/ppermute | solution.py:24
  153.7 13.8 %collective-permute-start.18 = (bf16[64,1664]{1,0:T(8,128)(2,1)S(1)}, bf16[64,1664]{1,0:T(8,128)(2,1)S(1)}, u32[]{:S(2)}, u32[]{:S(2)}) collective-permute-start(bf16[64,1664]{1,0:T(8,128)(2,1)S(1)} %get-tuple-element.21), channel_id=1, source_target_pairs={{0,448},{32,480},{64,0},{96,32},{128,64},{160,96},{192,128},{224,1... | collective-permute-start | bytes 638984 | tf_op jit(solution)/shard_map/ppermute | solution.py:24
  (4 other events, 22.4 us)

commit v2 on v1

v2 whole, which is shorter than its diff:
```python
import jax
import jax.numpy as jnp
import numpy as np
from jax import lax
from jax.experimental import pallas as pl
from jax.experimental.pallas import tpu as pltpu
from jax.sharding import Mesh, PartitionSpec as P

D = 16384
HAD = 128
UNITS = 1664
LANES = 128
EPSILON = 1e-05

AXES = ("zh", "zl", "xh", "y", "xl", "c")
SIZES = (4, 4, 2, 4, 2, 2)
GX = ("zh", "zl", "xh")
GY = ("y", "xl", "c")
Z = ("zh", "zl")
f32, bf16 = jnp.float32, jnp.bfloat16


def along_z(x, d):
    return lax.ppermute(x, Z, [(i, (i + d) % 16) for i in range(16)])


def two_along_z(x):
    return lax.ppermute(x, Z, [(i, (i + (-2 if i % 2 else 2)) % 16) for i in range(16)])


def across_x(x):
    return lax.ppermute(x, "xh", [(0, 1), (1, 0)])


def dot(a, b):
    return jnp.dot(a, b, preferred_element_type=f32)


def hadamard():
    i = np.arange(HAD)
    both = i[:, None] & i[None, :]
    parity = np.zeros_like(both)
    for bit in range(7):
        parity ^= (both >> bit) & 1
    return jnp.asarray(1.0 - 2.0 * parity, bf16)


def finish(own, a, b, c, signs, had, out):
    def total(lo, hi):
        return (own[:, lo:hi].astype(f32) + a[:, lo:hi].astype(f32)
                + b[:, lo:hi].astype(f32) + c[:, lo:hi].astype(f32))

    squares = jnp.sum(total(2 * UNITS, 2 * UNITS + LANES), axis=1, keepdims=True)
    inverse = lax.rsqrt(squares / D + EPSILON)
    for k in range(UNITS // HAD):
        lo = k * HAD
        gate = total(lo, lo + HAD) * inverse
        up = total(UNITS + lo, UNITS + lo + HAD) * inverse
        hidden = (gate / (1.0 + jnp.exp(-gate)) * up).astype(bf16)
        signed = hidden * signs[:, lo:lo + HAD]
        out[:, lo:lo + HAD] = (dot(signed, had[...]) * HAD ** (-0.5)).astype(bf16)


def local(tokens, gate_weight, up_weight, down_weight, sign_bits):
    zh, zl, xh = lax.axis_index("zh"), lax.axis_index("zl"), lax.axis_index("xh")

    sent = jnp.broadcast_to(tokens[None], (8, 32, 512))
    some = lax.all_to_all(sent, ("y", "xl"), 0, 0, tiled=True).reshape(256, 512)
    gathered = lax.all_gather(some, "c", axis=0, tiled=True)

    rows = gathered.reshape(4, 2, 64, 512)

    def gate_of(x):
        t = lax.dynamic_index_in_dim(rows, x, 1, keepdims=False).reshape(256, 512)
        return dot(t, gate_weight)

    def up_of(d, after=None):
        t = lax.dynamic_index_in_dim(rows, (zl + d) % 4, 0, keepdims=False).reshape(128, 512)
        if after is not None:
            t, _ = lax.optimization_barrier((t, after))
        v = t.astype(f32)
        v = v * v
        squares = v[:, :128] + v[:, 128:256] + v[:, 256:384] + v[:, 384:]
        return jnp.concatenate([dot(t, up_weight).astype(bf16), squares.astype(bf16)], axis=1)

    gate_out = gate_of(1 - xh).astype(bf16)
    gate_in = across_x(gate_out)
    up1 = up_of(1, gate_out)
    up_c = along_z(up1, 1)
    up3 = up_of(3, up1)
    up_d = along_z(up3, -1)
    up2 = up_of(2, up3)
    up_a = two_along_z(up2)
    up_own = up_of(0, up2).astype(f32)
    gate_own = gate_of(xh)

    gate = (gate_own + gate_in.astype(f32)).astype(bf16).reshape(4, 64, UNITS)

    def gate_class(d):
        return lax.dynamic_index_in_dim(gate, (zl + d) % 4, 0, keepdims=False)

    gate_c = along_z(gate_class(1), 1)
    gate_d = along_z(gate_class(3), -1)
    gate_a = two_along_z(gate_class(2))
    up = (up_own + up_c.astype(f32) + up_d.astype(f32) + up_a.astype(f32)).reshape(2, 64, UNITS + LANES)
    up_in = across_x(lax.dynamic_index_in_dim(up, 1 - xh, 0, keepdims=False).astype(bf16))
    up = lax.dynamic_index_in_dim(up, xh, 0, keepdims=False) + up_in.astype(f32)
    gate = gate_class(0).astype(f32) + gate_c.astype(f32) + gate_d.astype(f32) + gate_a.astype(f32)

    both = jnp.concatenate([gate.astype(bf16), up.astype(bf16)], axis=1).reshape(2, 4, 8, 2 * UNITS + LANES)

    def both_class(d):
        return lax.dynamic_index_in_dim(both, (zh + d) % 4, 1, keepdims=False).reshape(16, 2 * UNITS + LANES)

    far_a = along_z(both_class(1), 4)
    far_b = along_z(both_class(3), -4)
    far_c = along_z(both_class(2), 8)

    signs = (2 * sign_bits - 1).astype(bf16).reshape(1, UNITS)
    rotated = pl.pallas_call(
        finish,
        out_shape=jax.ShapeDtypeStruct((16, UNITS), bf16),
    )(both_class(0), far_a, far_b, far_c, signs, hadamard())

    far = lax.all_gather(rotated, "zh", axis=0, tiled=True)
    near = lax.all_gather(far, "xh", axis=0, tiled=True)
    n3 = along_z(near, 1)
    n1 = along_z(near, -1)
    n2 = two_along_z(near)
    pieces = [dot(v, down_weight).astype(bf16) for v in (near, n1, n2, n3)]
    out = jnp.concatenate(pieces, axis=0)

    r = lax.broadcasted_iota(jnp.int32, (512, 512), 1)
    d, x, far_z, half, k = r // 128, r // 64 % 2, r // 16 % 4, r // 8 % 2, r % 8
    place = ((((zl + d) % 4 * 2 + x) * 2 + half) * 4 + far_z) * 8 + k
    order = (place == lax.broadcasted_iota(jnp.int32, (512, 512), 0)).astype(bf16)
    out = dot(order, out).astype(bf16)

    parts = lax.all_to_all(out.reshape(16, 32, 512), ("c", "y", "xl"), 0, 0, tiled=True)
    return jnp.sum(parts.astype(f32), axis=0).astype(bf16)


def solution(mesh):
    fine = Mesh(mesh.devices.reshape(SIZES), AXES)
    return jax.shard_map(
        local,
        mesh=fine,
        in_specs=(P(GY, GX), P(GX, GY), P(GX, GY), P(GY, GX), P(GY)),
        out_specs=P(GY, GX),
        check_vma=False,
    )
```

time: 193 us -> 176 us (0.912)
  the two profiles are of different devices: /device:TPU:39 before, /device:TPU:1 now
where the time goes in v2:
time: 176 us; the launch traced here: 175 us
  waiting for transfers between devices  57.8 us (33%)
  starting transfers between devices  56.9 us (32%)
  blocking collectives  46.2 us (26%)
  matrix products  5.03 us (3%)
  local copies, waits for them, and re-layouts  3.78 us (2%)
  other arithmetic  3.22 us (2%)
  Pallas kernels  1.99 us (1%)
    ppermute x9, starting transfers between devices, along_z(): return lax.ppermute(x, Z, [(i, (i + d) % 16) for i in range(16)])  40.9 us
    ppermute x9, waiting for transfers between devices, along_z(): return lax.ppermute(x, Z, [(i, (i + d) % 16) for i in range(16)])  27.5 us
    ppermute x3, waiting for transfers between devices, two_along_z(): lax.ppermute(x, Z, [(i, (i + (-2 if i % 2 else 2)) % 16) for i in range(1...  26 us
    all_gather x1, blocking collectives, local(): far = lax.all_gather(rotated, 'zh', axis=0, tiled=True)  15.8 us
    all_to_all x1, blocking collectives, local(): lax.all_to_all(out.reshape(16, 32, 512), ('c', 'y', 'xl'), 0, 0, tiled=True)  15.5 us
    all_gather x1, blocking collectives, local(): gathered = lax.all_gather(some, 'c', axis=0, tiled=True)  8.05 us
    all_gather x1, blocking collectives, local(): near = lax.all_gather(far, 'xh', axis=0, tiled=True)  6.87 us
    all_to_all x1, starting transfers between devices, local(): some = lax.all_to_all(sent, ('y', 'xl'), 0, 0, tiled=True).reshape(256, 512)  5.95 us
  transfers between devices with their start and end apart: 15, of which 9 were waited for; matrix products, arithmetic and copies ran while one was open for 4% of the time, Pallas kernels for 0%

profile of v2, /device:TPU:1, one launch (start us, length us, event | category | flops | bytes accessed | tf_op | source)
XLA Modules:
  0.0 175.4 jit_solution(6159826810468603671)
XLA Ops:
  1.6 5.9 %all-to-all-start = ((bf16[8,32,512]{2,1,0:T(8,128)(2,1)}), bf16[8,32,512]{2,1,0:T(8,128)(2,1)}, u32[]{:S(2)}, u32[]{:S(2)}) async-start(bf16[8,32,512]{2,1,0:T(8,128)(2,1)} %broadcast_in_dim.2), calls=%async_computation | async-start | bytes 524288 | tf_op jit(solution)/shard_map/all_to_all | solution.py:68
  9.5 4.4 %all-to-all-done = bf16[8,32,512]{2,1,0:T(8,128)(2,1)} async-done(((bf16[8,32,512]{2,1,0:T(8,128)(2,1)}), bf16[8,32,512]{2,1,0:T(8,128)(2,1)}, u32[]{:S(2)}, u32[]{:S(2)}) %all-to-all-start) | async-done | bytes 262176 | tf_op jit(solution)/shard_map/all_to_all | solution.py:68
  13.8 8.1 %all_gather.9 = bf16[512,512]{1,0:T(8,128)(2,1)S(1)} all-gather(bf16[256,512]{1,0:T(8,128)(2,1)} %bitcast), channel_id=1, replica_groups=mesh['zh'=4,'zl'=4,'xh'=2,'y'=4,'xl'=2,'c'=2] {'c'}, dimensions={0}, use_global_device_ids=true | all-gather | bytes 786432 | tf_op jit(solution)/shard_map/all_gather | solution.py:69
  22.6 1.9 %collective-permute-start = (bf16[256,1664]{1,0:T(8,128)(2,1)S(1)}, bf16[256,1664]{1,0:T(8,128)(2,1)S(1)}, u32[]{:S(2)}, u32[]{:S(2)}) collective-permute-start(bf16[256,1664]{1,0:T(8,128)(2,1)S(1)} %convolution_convert_fusion), channel_id=1, source_target_pairs={{0,16},{16,0},{1,17},{17,1},{2,18},{18,2},{3,19},{19,3},{4,20},{20... | collective-permute-start | bytes 2555912 | tf_op jit(solution)/shard_map/ppermute | solution.py:32
  26.1 9.6 %collective-permute-start.5 = (bf16[128,1792]{1,0:T(8,128)(2,1)S(1)}, bf16[128,1792]{1,0:T(8,128)(2,1)S(1)}, u32[]{:S(2)}, u32[]{:S(2)}) collective-permute-start(bf16[128,1792]{1,0:T(8,128)(2,1)S(1)} %pad_maximum_fusion.1), channel_id=1, source_target_pairs={{0,480},{32,0},{64,32},{96,64},{128,96},{160,128},{192,160},{224,1... | collective-permute-start | bytes 1376264 | tf_op jit(solution)/shard_map/ppermute | solution.py:24
  35.7 1.9 %collective-permute-start.4 = (bf16[128,1792]{1,0:T(8,128)(2,1)S(1)}, bf16[128,1792]{1,0:T(8,128)(2,1)S(1)}, u32[]{:S(2)}, u32[]{:S(2)}) collective-permute-start(bf16[128,1792]{1,0:T(8,128)(2,1)S(1)} %pad_maximum_fusion), channel_id=1, source_target_pairs={{0,32},{32,64},{64,96},{96,128},{128,160},{160,192},{192,224},{224... | collective-permute-start | bytes 1376264 | tf_op jit(solution)/shard_map/ppermute | solution.py:24
  37.7 1.9 %collective-permute-start.6 = (bf16[128,1792]{1,0:T(8,128)(2,1)S(1)}, bf16[128,1792]{1,0:T(8,128)(2,1)S(1)}, u32[]{:S(2)}, u32[]{:S(2)}) collective-permute-start(bf16[128,1792]{1,0:T(8,128)(2,1)S(1)} %pad_maximum_fusion.2), channel_id=1, source_target_pairs={{0,64},{32,480},{64,128},{96,32},{128,192},{160,96},{192,256},{224... | collective-permute-start | bytes 1376264 | tf_op jit(solution)/shard_map/ppermute | solution.py:28
  40.1 18.9 %collective-permute-done.6 = bf16[128,1792]{1,0:T(8,128)(2,1)S(1)} collective-permute-done((bf16[128,1792]{1,0:T(8,128)(2,1)S(1)}, bf16[128,1792]{1,0:T(8,128)(2,1)S(1)}, u32[]{:S(2)}, u32[]{:S(2)}) %collective-permute-start.6) | collective-permute-done | bytes 458784 | tf_op jit(solution)/shard_map/ppermute | solution.py:28
  59.3 2.4 %collective-permute-start.7 = (bf16[64,1792]{1,0:T(8,128)(2,1)S(1)}, bf16[64,1792]{1,0:T(8,128)(2,1)S(1)}, u32[]{:S(2)}, u32[]{:S(2)}) collective-permute-start(bf16[64,1792]{1,0:T(8,128)(2,1)S(1)} %fusion.47), channel_id=1, source_target_pairs={{0,16},{16,0},{1,17},{17,1},{2,18},{18,2},{3,19},{19,3},{4,20},{20... | collective-permute-start | bytes 688136 | tf_op jit(solution)/shard_map/ppermute | solution.py:32
  62.4 1.9 %collective-permute-start.1 = (bf16[64,1664]{1,0:T(8,128)(2,1)S(1)}, bf16[64,1664]{1,0:T(8,128)(2,1)S(1)}, u32[]{:S(2)}, u32[]{:S(2)}) collective-permute-start(bf16[64,1664]{1,0:T(8,128)(2,1)S(1)} %get-tuple-element.13), channel_id=1, source_target_pairs={{0,32},{32,64},{64,96},{96,128},{128,160},{160,192},{192,224},{224... | collective-permute-start | bytes 638984 | tf_op jit(solution)/shard_map/ppermute | solution.py:24
  64.3 4.6 %collective-permute-start.2 = (bf16[64,1664]{1,0:T(8,128)(2,1)S(1)}, bf16[64,1664]{1,0:T(8,128)(2,1)S(1)}, u32[]{:S(2)}, u32[]{:S(2)}) collective-permute-start(bf16[64,1664]{1,0:T(8,128)(2,1)S(1)} %get-tuple-element.15), channel_id=1, source_target_pairs={{0,480},{32,0},{64,32},{96,64},{128,96},{160,128},{192,160},{224,1... | collective-permute-start | bytes 638984 | tf_op jit(solution)/shard_map/ppermute | solution.py:24
  71.7 5.9 %collective-permute-done.3 = bf16[64,1664]{1,0:T(8,128)(2,1)S(1)} collective-permute-done((bf16[64,1664]{1,0:T(8,128)(2,1)S(1)}, bf16[64,1664]{1,0:T(8,128)(2,1)S(1)}, u32[]{:S(2)}, u32[]{:S(2)}) %collective-permute-start.3) | collective-permute-done | bytes 213024 | tf_op jit(solution)/shard_map/ppermute | solution.py:28
  78.5 7.1 %collective-permute-start.10 = (bf16[16,3456]{1,0:T(8,128)(2,1)S(1)}, bf16[16,3456]{1,0:T(8,128)(2,1)S(1)}, u32[]{:S(2)}, u32[]{:S(2)}) collective-permute-start(bf16[16,3456]{1,0:T(8,128)(2,1)S(1)} %get-tuple-element.22), channel_id=1, source_target_pairs={{0,256},{32,288},{64,320},{96,352},{128,384},{160,416},{192,448},{... | collective-permute-start | bytes 331784 | tf_op jit(solution)/shard_map/ppermute | solution.py:24
  85.6 5.0 %collective-permute-start.8 = (bf16[16,3456]{1,0:T(8,128)(2,1)S(1)}, bf16[16,3456]{1,0:T(8,128)(2,1)S(1)}, u32[]{:S(2)}, u32[]{:S(2)}) collective-permute-start(bf16[16,3456]{1,0:T(8,128)(2,1)S(1)} %get-tuple-element.24), channel_id=1, source_target_pairs={{0,128},{32,160},{64,192},{96,224},{128,256},{160,288},{192,320},{... | collective-permute-start | bytes 331784 | tf_op jit(solution)/shard_map/ppermute | solution.py:24
  90.7 4.2 %collective-permute-start.9 = (bf16[16,3456]{1,0:T(8,128)(2,1)S(1)}, bf16[16,3456]{1,0:T(8,128)(2,1)S(1)}, u32[]{:S(2)}, u32[]{:S(2)}) collective-permute-start(bf16[16,3456]{1,0:T(8,128)(2,1)S(1)} %get-tuple-element.23), channel_id=1, source_target_pairs={{0,384},{32,416},{64,448},{96,480},{128,0},{160,32},{192,64},{224,... | collective-permute-start | bytes 331784 | tf_op jit(solution)/shard_map/ppermute | solution.py:24
  95.4 6.9 %collective-permute-done.8.a = bf16[16,3456]{1,0:T(8,128)(2,1)S(1)} collective-permute-done((bf16[16,3456]{1,0:T(8,128)(2,1)S(1)}, bf16[16,3456]{1,0:T(8,128)(2,1)S(1)}, u32[]{:S(2)}, u32[]{:S(2)}) %collective-permute-start.8) | collective-permute-done | bytes 110624 | tf_op jit(solution)/shard_map/ppermute | solution.py:24
  102.3 6.6 %collective-permute-done.9.b = bf16[16,3456]{1,0:T(8,128)(2,1)S(1)} collective-permute-done((bf16[16,3456]{1,0:T(8,128)(2,1)S(1)}, bf16[16,3456]{1,0:T(8,128)(2,1)S(1)}, u32[]{:S(2)}, u32[]{:S(2)}) %collective-permute-start.9) | collective-permute-done | bytes 110624 | tf_op jit(solution)/shard_map/ppermute | solution.py:24
  109.6 2.0 %shard_map.64 = bf16[16,1664]{1,0:T(8,128)(2,1)} custom-call(bf16[16,3456]{1,0:T(8,128)(2,1)} %get-tuple-element.25.own, bf16[16,3456]{1,0:T(8,128)(2,1)} %copy-done.4, bf16[16,3456]{1,0:T(8,128)(2,1)} %copy-done.5, bf16[16,3456]{1,0:T(8,128)(2,1)} %copy-done.3, bf16[1,1664]{1,0:T(2,128)(2,1)} %reshape.80.signs, bf16[128,128]{1,0:T(8,128)(2,1)} %constant.214.clone.had), custom_call_target="tpu_custom_call" | custom-call | tf_op jit(solution)/shard_map/pallas_call | solution.py:120
  111.6 15.8 %all_gather.10 = bf16[64,1664]{1,0:T(8,128)(2,1)S(1)} all-gather(bf16[16,1664]{1,0:T(8,128)(2,1)} %shard_map.64), channel_id=1, replica_groups=mesh['zh'=4,'zl'=4,'xh'=2,'y'=4,'xl'=2,'c'=2] {'zh'}, dimensions={0}, use_global_device_ids=true | all-gather | bytes 266240 | tf_op jit(solution)/shard_map/all_gather | solution.py:125
  127.3 6.9 %all_gather.11 = bf16[128,1664]{1,0:T(8,128)(2,1)S(1)} all-gather(bf16[64,1664]{1,0:T(8,128)(2,1)S(1)} %all_gather.10), channel_id=1, replica_groups=mesh['zh'=4,'zl'=4,'xh'=2,'y'=4,'xl'=2,'c'=2] {'xh'}, dimensions={0}, use_global_device_ids=true | all-gather | bytes 638976 | tf_op jit(solution)/shard_map/all_gather | solution.py:126
  138.1 4.6 %collective-permute-start.11 = (bf16[128,1664]{1,0:T(8,128)(2,1)S(1)}, bf16[128,1664]{1,0:T(8,128)(2,1)S(1)}, u32[]{:S(2)}, u32[]{:S(2)}) collective-permute-start(bf16[128,1664]{1,0:T(8,128)(2,1)S(1)} %all_gather.11), channel_id=1, source_target_pairs={{0,480},{32,0},{64,32},{96,64},{128,96},{160,128},{192,160},{224,1... | collective-permute-start | bytes 1277960 | tf_op jit(solution)/shard_map/ppermute | solution.py:24
  143.1 5.9 %collective-permute-done.13 = bf16[128,1664]{1,0:T(8,128)(2,1)S(1)} collective-permute-done((bf16[128,1664]{1,0:T(8,128)(2,1)S(1)}, bf16[128,1664]{1,0:T(8,128)(2,1)S(1)}, u32[]{:S(2)}, u32[]{:S(2)}) %collective-permute-start.13) | collective-permute-done | bytes 426016 | tf_op jit(solution)/shard_map/ppermute | solution.py:24
  151.0 7.3 %collective-permute-done.11 = bf16[128,1664]{1,0:T(8,128)(2,1)S(1)} collective-permute-done((bf16[128,1664]{1,0:T(8,128)(2,1)S(1)}, bf16[128,1664]{1,0:T(8,128)(2,1)S(1)}, u32[]{:S(2)}, u32[]{:S(2)}) %collective-permute-start.11) | collective-permute-done | bytes 426016 | tf_op jit(solution)/shard_map/ppermute | solution.py:24
  159.2 15.5 %all_to_all.10 = bf16[16,32,512]{2,1,0:T(8,128)(2,1)S(1)} all-to-all(bf16[16,32,512]{2,1,0:T(8,128)(2,1)S(1)} %bitcast.72), channel_id=1, replica_groups=mesh['zh'=4,'zl'=4,'xh'=2,'y'=4,'xl'=2,'c'=2] {'c','y','xl'}, dimensions={0} | all-to-all | bytes 1048576 | tf_op jit(solution)/shard_map/all_to_all | solution.py:139
  (72 shorter events, 19.7 us)
Async XLA Ops:
  0.0 24.6 %copy-start = (bf16[512,1664]{1,0:T(8,128)(2,1)S(1)}, bf16[512,1664]{1,0:T(8,128)(2,1)}, u32[]{:S(2)}) copy-start(bf16[512,1664]{1,0:T(8,128)(2,1)} %param.8) | copy-start | bytes 5111812
  0.0 21.9 %copy-start.2 = (bf16[512,1664]{1,0:T(8,128)(2,1)S(1)}, bf16[512,1664]{1,0:T(8,128)(2,1)}, u32[]{:S(2)}) copy-start(bf16[512,1664]{1,0:T(8,128)(2,1)} %param.7) | copy-start | bytes 5111812
  1.6 12.2 %all-to-all-start = ((bf16[8,32,512]{2,1,0:T(8,128)(2,1)}), bf16[8,32,512]{2,1,0:T(8,128)(2,1)}, u32[]{:S(2)}, u32[]{:S(2)}) async-start(bf16[8,32,512]{2,1,0:T(8,128)(2,1)} %broadcast_in_dim.2), calls=%async_computation | async-start | bytes 524288 | tf_op jit(solution)/shard_map/all_to_all | solution.py:68
  22.6 39.1 %collective-permute-start = (bf16[256,1664]{1,0:T(8,128)(2,1)S(1)}, bf16[256,1664]{1,0:T(8,128)(2,1)S(1)}, u32[]{:S(2)}, u32[]{:S(2)}) collective-permute-start(bf16[256,1664]{1,0:T(8,128)(2,1)S(1)} %convolution_convert_fusion), channel_id=1, source_target_pairs={{0,16},{16,0},{1,17},{17,1},{2,18},{18,2},{3,19},{19,3},{4,20},{20... | collective-permute-start | bytes 2555912 | tf_op jit(solution)/shard_map/ppermute | solution.py:32
  26.1 32.9 %collective-permute-start.5 = (bf16[128,1792]{1,0:T(8,128)(2,1)S(1)}, bf16[128,1792]{1,0:T(8,128)(2,1)S(1)}, u32[]{:S(2)}, u32[]{:S(2)}) collective-permute-start(bf16[128,1792]{1,0:T(8,128)(2,1)S(1)} %pad_maximum_fusion.1), channel_id=1, source_target_pairs={{0,480},{32,0},{64,32},{96,64},{128,96},{160,128},{192,160},{224,1... | collective-permute-start | bytes 1376264 | tf_op jit(solution)/shard_map/ppermute | solution.py:24
  35.7 23.3 %collective-permute-start.4 = (bf16[128,1792]{1,0:T(8,128)(2,1)S(1)}, bf16[128,1792]{1,0:T(8,128)(2,1)S(1)}, u32[]{:S(2)}, u32[]{:S(2)}) collective-permute-start(bf16[128,1792]{1,0:T(8,128)(2,1)S(1)} %pad_maximum_fusion), channel_id=1, source_target_pairs={{0,32},{32,64},{64,96},{96,128},{128,160},{160,192},{192,224},{224... | collective-permute-start | bytes 1376264 | tf_op jit(solution)/shard_map/ppermute | solution.py:24
  37.7 21.3 %collective-permute-start.6 = (bf16[128,1792]{1,0:T(8,128)(2,1)S(1)}, bf16[128,1792]{1,0:T(8,128)(2,1)S(1)}, u32[]{:S(2)}, u32[]{:S(2)}) collective-permute-start(bf16[128,1792]{1,0:T(8,128)(2,1)S(1)} %pad_maximum_fusion.2), channel_id=1, source_target_pairs={{0,64},{32,480},{64,128},{96,32},{128,192},{160,96},{192,256},{224... | collective-permute-start | bytes 1376264 | tf_op jit(solution)/shard_map/ppermute | solution.py:28
  59.3 11.6 %collective-permute-start.7 = (bf16[64,1792]{1,0:T(8,128)(2,1)S(1)}, bf16[64,1792]{1,0:T(8,128)(2,1)S(1)}, u32[]{:S(2)}, u32[]{:S(2)}) collective-permute-start(bf16[64,1792]{1,0:T(8,128)(2,1)S(1)} %fusion.47), channel_id=1, source_target_pairs={{0,16},{16,0},{1,17},{17,1},{2,18},{18,2},{3,19},{19,3},{4,20},{20... | collective-permute-start | bytes 688136 | tf_op jit(solution)/shard_map/ppermute | solution.py:32
  62.4 8.5 %collective-permute-start.1 = (bf16[64,1664]{1,0:T(8,128)(2,1)S(1)}, bf16[64,1664]{1,0:T(8,128)(2,1)S(1)}, u32[]{:S(2)}, u32[]{:S(2)}) collective-permute-start(bf16[64,1664]{1,0:T(8,128)(2,1)S(1)} %get-tuple-element.13), channel_id=1, source_target_pairs={{0,32},{32,64},{64,96},{96,128},{128,160},{160,192},{192,224},{224... | collective-permute-start | bytes 638984 | tf_op jit(solution)/shard_map/ppermute | solution.py:24
  64.3 7.3 %collective-permute-start.2 = (bf16[64,1664]{1,0:T(8,128)(2,1)S(1)}, bf16[64,1664]{1,0:T(8,128)(2,1)S(1)}, u32[]{:S(2)}, u32[]{:S(2)}) collective-permute-start(bf16[64,1664]{1,0:T(8,128)(2,1)S(1)} %get-tuple-element.15), channel_id=1, source_target_pairs={{0,480},{32,0},{64,32},{96,64},{128,96},{160,128},{192,160},{224,1... | collective-permute-start | bytes 638984 | tf_op jit(solution)/shard_map/ppermute | solution.py:24
  68.9 8.7 %collective-permute-start.3 = (bf16[64,1664]{1,0:T(8,128)(2,1)S(1)}, bf16[64,1664]{1,0:T(8,128)(2,1)S(1)}, u32[]{:S(2)}, u32[]{:S(2)}) collective-permute-start(bf16[64,1664]{1,0:T(8,128)(2,1)S(1)} %get-tuple-element.14), channel_id=1, source_target_pairs={{0,64},{32,480},{64,128},{96,32},{128,192},{160,96},{192,256},{224... | collective-permute-start | bytes 638984 | tf_op jit(solution)/shard_map/ppermute | solution.py:28
  77.7 64.9 %copy-start.1 = (bf16[1664,512]{1,0:T(8,128)(2,1)S(1)}, bf16[1664,512]{1,0:T(8,128)(2,1)}, u32[]{:S(2)}) copy-start(bf16[1664,512]{1,0:T(8,128)(2,1)} %param.9) | copy-start | bytes 5111812
  78.5 16.9 %collective-permute-start.10 = (bf16[16,3456]{1,0:T(8,128)(2,1)S(1)}, bf16[16,3456]{1,0:T(8,128)(2,1)S(1)}, u32[]{:S(2)}, u32[]{:S(2)}) collective-permute-start(bf16[16,3456]{1,0:T(8,128)(2,1)S(1)} %get-tuple-element.22), channel_id=1, source_target_pairs={{0,256},{32,288},{64,320},{96,352},{128,384},{160,416},{192,448},{... | collective-permute-start | bytes 331784 | tf_op jit(solution)/shard_map/ppermute | solution.py:24
  85.6 16.7 %collective-permute-start.8 = (bf16[16,3456]{1,0:T(8,128)(2,1)S(1)}, bf16[16,3456]{1,0:T(8,128)(2,1)S(1)}, u32[]{:S(2)}, u32[]{:S(2)}) collective-permute-start(bf16[16,3456]{1,0:T(8,128)(2,1)S(1)} %get-tuple-element.24), channel_id=1, source_target_pairs={{0,128},{32,160},{64,192},{96,224},{128,256},{160,288},{192,320},{... | collective-permute-start | bytes 331784 | tf_op jit(solution)/shard_map/ppermute | solution.py:24
  90.7 18.2 %collective-permute-start.9 = (bf16[16,3456]{1,0:T(8,128)(2,1)S(1)}, bf16[16,3456]{1,0:T(8,128)(2,1)S(1)}, u32[]{:S(2)}, u32[]{:S(2)}) collective-permute-start(bf16[16,3456]{1,0:T(8,128)(2,1)S(1)} %get-tuple-element.23), channel_id=1, source_target_pairs={{0,384},{32,416},{64,448},{96,480},{128,0},{160,32},{192,64},{224,... | collective-permute-start | bytes 331784 | tf_op jit(solution)/shard_map/ppermute | solution.py:24
  95.4 14.1 %copy-start.3 = (bf16[16,3456]{1,0:T(8,128)(2,1)}, bf16[16,3456]{1,0:T(8,128)(2,1)S(1)}, u32[]{:S(2)}) copy-start(bf16[16,3456]{1,0:T(8,128)(2,1)S(1)} %collective-permute-done.10.c) | copy-start | bytes 331780
  102.3 6.6 %copy-start.4 = (bf16[16,3456]{1,0:T(8,128)(2,1)}, bf16[16,3456]{1,0:T(8,128)(2,1)S(1)}, u32[]{:S(2)}) copy-start(bf16[16,3456]{1,0:T(8,128)(2,1)S(1)} %collective-permute-done.8.a) | copy-start | bytes 331780
  108.9 0.6 copy-start.5
  134.2 14.8 %collective-permute-start.13 = (bf16[128,1664]{1,0:T(8,128)(2,1)S(1)}, bf16[128,1664]{1,0:T(8,128)(2,1)S(1)}, u32[]{:S(2)}, u32[]{:S(2)}) collective-permute-start(bf16[128,1664]{1,0:T(8,128)(2,1)S(1)} %all_gather.11), channel_id=1, source_target_pairs={{0,32},{32,64},{64,96},{96,128},{128,160},{160,192},{192,224},{224... | collective-permute-start | bytes 1277960 | tf_op jit(solution)/shard_map/ppermute | solution.py:24
  136.1 14.4 %collective-permute-start.12 = (bf16[128,1664]{1,0:T(8,128)(2,1)S(1)}, bf16[128,1664]{1,0:T(8,128)(2,1)S(1)}, u32[]{:S(2)}, u32[]{:S(2)}) collective-permute-start(bf16[128,1664]{1,0:T(8,128)(2,1)S(1)} %all_gather.11), channel_id=1, source_target_pairs={{0,64},{32,480},{64,128},{96,32},{128,192},{160,96},{192,256},{224... | collective-permute-start | bytes 1277960 | tf_op jit(solution)/shard_map/ppermute | solution.py:28
  138.1 20.3 %collective-permute-start.11 = (bf16[128,1664]{1,0:T(8,128)(2,1)S(1)}, bf16[128,1664]{1,0:T(8,128)(2,1)S(1)}, u32[]{:S(2)}, u32[]{:S(2)}) collective-permute-start(bf16[128,1664]{1,0:T(8,128)(2,1)S(1)} %all_gather.11), channel_id=1, source_target_pairs={{0,480},{32,0},{64,32},{96,64},{128,96},{160,128},{192,160},{224,1... | collective-permute-start | bytes 1277960 | tf_op jit(solution)/shard_map/ppermute | solution.py:24
  150.9 7.8 %copy-start.6 = (pred[512]{0:T(512)(128)(4,1)S(1)}, pred[512]{0:T(512)(128)(4,1)}, u32[]{:S(2)}) copy-start(pred[512]{0:T(512)(128)(4,1)} %get-tuple-element.27) | copy-start | bytes 1540
  151.0 7.8 %copy-start.7 = (pred[512]{0:T(512)(128)(4,1)S(1)}, pred[512]{0:T(512)(128)(4,1)}, u32[]{:S(2)}) copy-start(pred[512]{0:T(512)(128)(4,1)} %get-tuple-element.28) | copy-start | bytes 1540
  151.0 7.8 %copy-start.8 = (pred[512]{0:T(512)(128)(4,1)S(1)}, pred[512]{0:T(512)(128)(4,1)}, u32[]{:S(2)}) copy-start(pred[512]{0:T(512)(128)(4,1)} %get-tuple-element.29) | copy-start | bytes 1540

commit v3 on v2

v3 whole, which is shorter than its diff:
```python
import jax
import jax.numpy as jnp
from jax import lax
from jax.experimental import pallas as pl
from jax.experimental.pallas import tpu as pltpu
from jax.sharding import Mesh, PartitionSpec as P

D = 16384
HAD = 128
UNITS = 1664
LANES = 128
EPSILON = 1e-05

AXES = ("zh", "zl", "xh", "y", "xl", "c")
SIZES = (4, 4, 2, 4, 2, 2)
GX = ("zh", "zl", "xh")
GY = ("y", "xl", "c")
Z = ("zh", "zl")
f32, bf16 = jnp.float32, jnp.bfloat16


def along_z(x, d):
    return lax.ppermute(x, Z, [(i, (i + d) % 16) for i in range(16)])


def two_along_z(x):
    return lax.ppermute(x, Z, [(i, (i + (-2 if i % 2 else 2)) % 16) for i in range(16)])


def across_x(x):
    return lax.ppermute(x, "xh", [(0, 1), (1, 0)])


def dot(a, b):
    return jnp.dot(a, b, preferred_element_type=f32)


def finish(own, a, b, c, sign_bits, out):
    def total(lo, hi):
        return (own[:, lo:hi].astype(f32) + a[:, lo:hi].astype(f32)
                + b[:, lo:hi].astype(f32) + c[:, lo:hi].astype(f32))

    both = lax.broadcasted_iota(jnp.int32, (HAD, HAD), 0) & lax.broadcasted_iota(jnp.int32, (HAD, HAD), 1)
    both = both ^ (both >> 4)
    both = both ^ (both >> 2)
    both = both ^ (both >> 1)
    had = (1 - 2 * (both & 1)).astype(f32).astype(bf16)
    squares = jnp.sum(total(UNITS, UNITS + LANES), axis=1, keepdims=True)
    inverse = lax.rsqrt(squares / D + EPSILON)
    for k in range(UNITS // HAD):
        lo = k * HAD
        gate = total(lo, lo + HAD) * inverse
        up = total(UNITS + LANES + lo, UNITS + LANES + lo + HAD) * inverse
        hidden = (gate / (1.0 + jnp.exp(-gate)) * up).astype(bf16)
        signed = (hidden.astype(f32) * (2 * sign_bits[:, lo:lo + HAD] - 1).astype(f32)).astype(bf16)
        out[:, lo:lo + HAD] = (dot(signed, had) * HAD ** (-0.5)).astype(bf16)


def local(tokens, gate_weight, up_weight, down_weight, sign_bits):
    zh, zl, xh = lax.axis_index("zh"), lax.axis_index("zl"), lax.axis_index("xh")

    def pick(x, i, axis):
        return lax.dynamic_index_in_dim(x, i, axis, keepdims=False)

    sent = jnp.broadcast_to(tokens[None], (8, 32, 512))
    some = lax.all_to_all(sent, ("y", "xl"), 0, 0, tiled=True).reshape(256, 512)
    gathered = lax.all_gather(some, "c", axis=0, tiled=True)

    rows = gathered.reshape(2, 8, 4, 8, 512)

    def gate_of(x, after):
        t = pick(rows, x, 0).reshape(256, 512)
        t, _ = lax.optimization_barrier((t, after))
        v = t.astype(f32)
        v = v * v
        squares = v[:, :128] + v[:, 128:256] + v[:, 256:384] + v[:, 384:]
        return jnp.concatenate([dot(t, gate_weight), squares], axis=1)

    def up_of(d, after):
        t = pick(rows, (zl + d) & 3, 2).reshape(128, 512)
        t, _ = lax.optimization_barrier((t, after))
        return dot(t, up_weight).astype(bf16)

    up1 = up_of(1, tokens)
    up_c = along_z(up1, 1)
    up3 = up_of(3, up1)
    up_d = along_z(up3, -1)
    gate_out = gate_of(1 - xh, up3).astype(bf16)
    gate_in = across_x(gate_out)
    up2 = up_of(2, gate_out)
    up_a = two_along_z(up2)
    up_own = up_of(0, up2).astype(f32)
    gate_own = gate_of(xh, up2)

    gate = (gate_own + gate_in.astype(f32)).astype(bf16).reshape(8, 4, 8, UNITS + LANES)

    def gate_class(d):
        return pick(gate, (zl + d) & 3, 1).reshape(64, UNITS + LANES)

    gate_c = along_z(gate_class(1), 1)
    gate_d = along_z(gate_class(3), -1)
    gate_a = two_along_z(gate_class(2))
    up = (up_own + up_c.astype(f32) + up_d.astype(f32) + up_a.astype(f32)).reshape(2, 64, UNITS)
    up_in = across_x(pick(up, 1 - xh, 0).astype(bf16))
    up = pick(up, xh, 0) + up_in.astype(f32)
    gate = gate_class(0).astype(f32) + gate_c.astype(f32) + gate_d.astype(f32) + gate_a.astype(f32)

    both = jnp.concatenate([gate.astype(bf16), up.astype(bf16)], axis=1).reshape(4, 16, 2 * UNITS + LANES)
    far_a = along_z(pick(both, (zh + 1) & 3, 0), 4)
    far_b = along_z(pick(both, (zh + 3) & 3, 0), -4)
    far_c = along_z(pick(both, (zh + 2) & 3, 0), 8)

    rotated = pl.pallas_call(
        finish,
        out_shape=jax.ShapeDtypeStruct((16, UNITS), bf16),
        compiler_params=pltpu.CompilerParams(vmem_limit_bytes=4 * 1024 * 1024),
    )(pick(both, zh, 0), far_a, far_b, far_c, sign_bits.reshape(1, UNITS))

    mine = lax.all_gather(rotated, "zh", axis=0, tiled=True)
    theirs = across_x(mine)

    def from_near(v):
        return v, along_z(v, -1), two_along_z(v), along_z(v, 1)

    def out_of(v):
        return dot(v, down_weight).astype(bf16).reshape(8, 8, 512)

    own = [out_of(v) for v in from_near(mine)]
    other = [out_of(v) for v in from_near(theirs)]
    first = jnp.concatenate([jnp.where(xh == 0, p, q) for p, q in zip(own, other)], axis=1)
    second = jnp.concatenate([jnp.where(xh == 0, q, p) for p, q in zip(own, other)], axis=1)
    parts = lax.all_to_all(jnp.concatenate([first, second], axis=0), ("c", "y", "xl"), 0, 0, tiled=True)
    out = jnp.sum(parts.astype(f32), axis=0).astype(bf16)

    out = jnp.concatenate([out, out], axis=0)
    return lax.dynamic_slice_in_dim(out, ((4 - zl) & 3) * 8, 32, 0)


def solution(mesh):
    fine = Mesh(mesh.devices.reshape(SIZES), AXES)
    return jax.shard_map(
        local,
        mesh=fine,
        in_specs=(P(GY, GX), P(GX, GY), P(GX, GY), P(GY, GX), P(GY)),
        out_specs=P(GY, GX),
        check_vma=False,
    )
```

time: 176 us -> 172 us (0.977)
  starting transfers between devices: 56.9 us -> 84.2 us
  blocking collectives: 46.2 us -> 26.8 us
  waiting for transfers between devices: 57.8 us -> 47.4 us
  matrix products: 5.03 us -> 8.14 us
  local copies, waits for them, and re-layouts: 3.78 us -> 1.9 us
    all_to_all x1 -> x0, blocking collectives: 15.5 us -> none  [local(): lax.all_to_all(out.reshape(16, 32, 512), ('c', 'y', 'xl'), 0, 0, tiled=True)]
    ppermute x9 -> x11, waiting for transfers between devices: 27.5 us -> 13.4 us  [along_z(): return lax.ppermute(x, Z, [(i, (i + d) % 16) for i in range(16)])]
    ppermute x3 -> x4, waiting for transfers between devices: 26 us -> 15.9 us  [two_along_z(): lax.ppermute(x, Z, [(i, (i + (-2 if i % 2 else 2)) % 16) for i in range(1...]
    all_to_all x0 -> x1, waiting for transfers between devices: none -> 9.4 us  [local(): lax.all_to_all(jnp.concatenate([first, second], axis=0), ('c', 'y', 'xl')...]
    ppermute x2 -> x3, starting transfers between devices: 4.35 us -> 13 us  [across_x(): return lax.ppermute(x, 'xh', [(0, 1), (1, 0)])]
    all_to_all x0 -> x1, starting transfers between devices: none -> 6.85 us  [local(): lax.all_to_all(jnp.concatenate([first, second], axis=0), ('c', 'y', 'xl')...]
    ppermute x9 -> x11, starting transfers between devices: 40.9 us -> 47.5 us  [along_z(): return lax.ppermute(x, Z, [(i, (i + d) % 16) for i in range(16)])]
    ppermute x3 -> x4, starting transfers between devices: 5.76 us -> 10.9 us  [two_along_z(): lax.ppermute(x, Z, [(i, (i + (-2 if i % 2 else 2)) % 16) for i in range(1...]
  transfers between devices with their start and end apart: 15 -> 20, of which waited for: 9 -> 9; matrix products, arithmetic and copies ran while one was open for 4% -> 5% of each run, Pallas kernels for 0% -> 0%
where the time goes in v3:
time: 172 us
  starting transfers between devices  84.2 us (49%)
  waiting for transfers between devices  47.4 us (28%)
  blocking collectives  26.8 us (16%)
  matrix products  8.14 us (5%)
  other arithmetic  2.21 us (1%)
  local copies, waits for them, and re-layouts  1.9 us (1%)
    ppermute x11, starting transfers between devices, along_z(): return lax.ppermute(x, Z, [(i, (i + d) % 16) for i in range(16)])  47.5 us
    all_gather x1, blocking collectives, local(): mine = lax.all_gather(rotated, 'zh', axis=0, tiled=True)  18.8 us
    ppermute x4, waiting for transfers between devices, two_along_z(): lax.ppermute(x, Z, [(i, (i + (-2 if i % 2 else 2)) % 16) for i in range(1...  15.9 us
    ppermute x11, waiting for transfers between devices, along_z(): return lax.ppermute(x, Z, [(i, (i + d) % 16) for i in range(16)])  13.4 us
    ppermute x3, starting transfers between devices, across_x(): return lax.ppermute(x, 'xh', [(0, 1), (1, 0)])  13 us
    ppermute x4, starting transfers between devices, two_along_z(): lax.ppermute(x, Z, [(i, (i + (-2 if i % 2 else 2)) % 16) for i in range(1...  10.9 us
    all_to_all x1, waiting for transfers between devices, local(): lax.all_to_all(jnp.concatenate([first, second], axis=0), ('c', 'y', 'xl')...  9.4 us
    dot_general x14, matrix products, dot(): return jnp.dot(a, b, preferred_element_type=f32)  8.14 us
  transfers between devices with their start and end apart: 20, of which 9 were waited for; matrix products, arithmetic and copies ran while one was open for 5% of the time, Pallas kernels for 0%

profile of v3, /device:TPU:1, one launch (start us, length us, event | category | flops | bytes accessed | tf_op | source)
XLA Modules:
  0.0 171.5 jit_solution(13721660734843298077)
XLA Ops:
  1.6 5.9 %all-to-all-start = ((bf16[8,32,512]{2,1,0:T(8,128)(2,1)}), bf16[8,32,512]{2,1,0:T(8,128)(2,1)}, u32[]{:S(2)}, u32[]{:S(2)}) async-start(bf16[8,32,512]{2,1,0:T(8,128)(2,1)} %broadcast_in_dim.2), calls=%async_computation | async-start | bytes 524288 | tf_op jit(solution)/shard_map/all_to_all | solution.py:66
  7.6 6.2 %all-to-all-done = bf16[8,32,512]{2,1,0:T(8,128)(2,1)} async-done(((bf16[8,32,512]{2,1,0:T(8,128)(2,1)}), bf16[8,32,512]{2,1,0:T(8,128)(2,1)}, u32[]{:S(2)}, u32[]{:S(2)}) %all-to-all-start) | async-done | bytes 262176 | tf_op jit(solution)/shard_map/all_to_all | solution.py:66
  13.8 8.0 %all_gather.6 = bf16[512,512]{1,0:T(8,128)(2,1)S(1)} all-gather(bf16[256,512]{1,0:T(8,128)(2,1)} %bitcast), channel_id=1, replica_groups=mesh['zh'=4,'zl'=4,'xh'=2,'y'=4,'xl'=2,'c'=2] {'c'}, dimensions={0}, use_global_device_ids=true | all-gather | bytes 786432 | tf_op jit(solution)/shard_map/all_gather | solution.py:67
  24.7 7.2 %collective-permute-start.5 = (bf16[128,1664]{1,0:T(8,128)(2,1)S(1)}, bf16[128,1664]{1,0:T(8,128)(2,1)S(1)}, u32[]{:S(2)}, u32[]{:S(2)}) collective-permute-start(bf16[128,1664]{1,0:T(8,128)(2,1)S(1)} %convolution_convert_fusion.3), channel_id=1, source_target_pairs={{0,480},{32,0},{64,32},{96,64},{128,96},{160,128},{192,160},{224,1... | collective-permute-start | bytes 1277960 | tf_op jit(solution)/shard_map/ppermute | solution.py:23
  32.8 4.4 %collective-permute-start = (bf16[256,1792]{1,0:T(8,128)(2,1)S(1)}, bf16[256,1792]{1,0:T(8,128)(2,1)S(1)}, u32[]{:S(2)}, u32[]{:S(2)}) collective-permute-start(bf16[256,1792]{1,0:T(8,128)(2,1)S(1)} %pad_maximum_fusion), channel_id=1, source_target_pairs={{0,16},{16,0},{1,17},{17,1},{2,18},{18,2},{3,19},{19,3},{4,20},{20... | collective-permute-start | bytes 2752520 | tf_op jit(solution)/shard_map/ppermute | solution.py:31
  40.7 11.3 %collective-permute-done.6 = bf16[128,1664]{1,0:T(8,128)(2,1)S(1)} collective-permute-done((bf16[128,1664]{1,0:T(8,128)(2,1)S(1)}, bf16[128,1664]{1,0:T(8,128)(2,1)S(1)}, u32[]{:S(2)}, u32[]{:S(2)}) %collective-permute-start.6) | collective-permute-done | bytes 426016 | tf_op jit(solution)/shard_map/ppermute | solution.py:27
  52.5 2.4 %collective-permute-start.7 = (bf16[64,1664]{1,0:T(8,128)(2,1)S(1)}, bf16[64,1664]{1,0:T(8,128)(2,1)S(1)}, u32[]{:S(2)}, u32[]{:S(2)}) collective-permute-start(bf16[64,1664]{1,0:T(8,128)(2,1)S(1)} %fusion.6), channel_id=1, source_target_pairs={{0,16},{16,0},{1,17},{17,1},{2,18},{18,2},{3,19},{19,3},{4,20},{20... | collective-permute-start | bytes 638984 | tf_op jit(solution)/shard_map/ppermute | solution.py:31
  54.9 2.5 %collective-permute-done = bf16[256,1792]{1,0:T(8,128)(2,1)S(1)} collective-permute-done((bf16[256,1792]{1,0:T(8,128)(2,1)S(1)}, bf16[256,1792]{1,0:T(8,128)(2,1)S(1)}, u32[]{:S(2)}, u32[]{:S(2)}) %collective-permute-start) | collective-permute-done | bytes 917536 | tf_op jit(solution)/shard_map/ppermute | solution.py:31
  57.7 1.9 %collective-permute-start.1 = (bf16[64,1792]{1,0:T(8,128)(2,1)S(1)}, bf16[64,1792]{1,0:T(8,128)(2,1)S(1)}, u32[]{:S(2)}, u32[]{:S(2)}) collective-permute-start(bf16[64,1792]{1,0:T(8,128)(2,1)S(1)} %get-tuple-element.17), channel_id=1, source_target_pairs={{0,32},{32,64},{64,96},{96,128},{128,160},{160,192},{192,224},{224... | collective-permute-start | bytes 688136 | tf_op jit(solution)/shard_map/ppermute | solution.py:23
  61.5 4.9 %collective-permute-start.2 = (bf16[64,1792]{1,0:T(8,128)(2,1)S(1)}, bf16[64,1792]{1,0:T(8,128)(2,1)S(1)}, u32[]{:S(2)}, u32[]{:S(2)}) collective-permute-start(bf16[64,1792]{1,0:T(8,128)(2,1)S(1)} %get-tuple-element.19), channel_id=1, source_target_pairs={{0,480},{32,0},{64,32},{96,64},{128,96},{160,128},{192,160},{224,1... | collective-permute-start | bytes 688136 | tf_op jit(solution)/shard_map/ppermute | solution.py:23
  66.5 4.6 %collective-permute-done.3 = bf16[64,1792]{1,0:T(8,128)(2,1)S(1)} collective-permute-done((bf16[64,1792]{1,0:T(8,128)(2,1)S(1)}, bf16[64,1792]{1,0:T(8,128)(2,1)S(1)}, u32[]{:S(2)}, u32[]{:S(2)}) %collective-permute-start.3) | collective-permute-done | bytes 229408 | tf_op jit(solution)/shard_map/ppermute | solution.py:27
  71.1 2.9 %collective-permute-done.2 = bf16[64,1792]{1,0:T(8,128)(2,1)S(1)} collective-permute-done((bf16[64,1792]{1,0:T(8,128)(2,1)S(1)}, bf16[64,1792]{1,0:T(8,128)(2,1)S(1)}, u32[]{:S(2)}, u32[]{:S(2)}) %collective-permute-start.2) | collective-permute-done | bytes 229408 | tf_op jit(solution)/shard_map/ppermute | solution.py:23
  74.3 8.9 %collective-permute-start.10 = (bf16[16,3456]{1,0:T(8,128)(2,1)S(1)}, bf16[16,3456]{1,0:T(8,128)(2,1)S(1)}, u32[]{:S(2)}, u32[]{:S(2)}) collective-permute-start(bf16[16,3456]{1,0:T(8,128)(2,1)S(1)} %get-tuple-element.26), channel_id=1, source_target_pairs={{0,256},{32,288},{64,320},{96,352},{128,384},{160,416},{192,448},{... | collective-permute-start | bytes 331784 | tf_op jit(solution)/shard_map/ppermute | solution.py:23
  85.1 7.3 %collective-permute-start.8 = (bf16[16,3456]{1,0:T(8,128)(2,1)S(1)}, bf16[16,3456]{1,0:T(8,128)(2,1)S(1)}, u32[]{:S(2)}, u32[]{:S(2)}) collective-permute-start(bf16[16,3456]{1,0:T(8,128)(2,1)S(1)} %get-tuple-element.28), channel_id=1, source_target_pairs={{0,128},{32,160},{64,192},{96,224},{128,256},{160,288},{192,320},{... | collective-permute-start | bytes 331784 | tf_op jit(solution)/shard_map/ppermute | solution.py:23
  92.5 8.6 %collective-permute-done.9.b = bf16[16,3456]{1,0:T(8,128)(2,1)S(1)} collective-permute-done((bf16[16,3456]{1,0:T(8,128)(2,1)S(1)}, bf16[16,3456]{1,0:T(8,128)(2,1)S(1)}, u32[]{:S(2)}, u32[]{:S(2)}) %collective-permute-start.9) | collective-permute-done | bytes 110624 | tf_op jit(solution)/shard_map/ppermute | solution.py:23
  101.4 18.8 %all_gather.7 = bf16[64,1664]{1,0:T(8,128)(2,1)} all-gather(bf16[16,1664]{1,0:T(8,128)(2,1)S(1)} %shard_map.55), channel_id=1, replica_groups=mesh['zh'=4,'zl'=4,'xh'=2,'y'=4,'xl'=2,'c'=2] {'zh'}, dimensions={0}, use_global_device_ids=true | all-gather | bytes 266240 | tf_op jit(solution)/shard_map/all_gather | solution.py:119
  120.2 6.2 %collective-permute-start.11 = (bf16[64,1664]{1,0:T(8,128)(2,1)}, bf16[64,1664]{1,0:T(8,128)(2,1)}, u32[]{:S(2)}, u32[]{:S(2)}) collective-permute-start(bf16[64,1664]{1,0:T(8,128)(2,1)} %all_gather.7), channel_id=1, source_target_pairs={{0,16},{16,0},{1,17},{17,1},{2,18},{18,2},{3,19},{19,3},{4,20},{20... | collective-permute-start | bytes 638984 | tf_op jit(solution)/shard_map/ppermute | solution.py:31
  128.3 2.6 %collective-permute-start.14 = (bf16[64,1664]{1,0:T(8,128)(2,1)}, bf16[64,1664]{1,0:T(8,128)(2,1)S(1)}, u32[]{:S(2)}, u32[]{:S(2)}) collective-permute-start(bf16[64,1664]{1,0:T(8,128)(2,1)} %all_gather.7), channel_id=1, source_target_pairs={{0,64},{32,480},{64,128},{96,32},{128,192},{160,96},{192,256},{224... | collective-permute-start | bytes 638984 | tf_op jit(solution)/shard_map/ppermute | solution.py:27
  130.9 4.7 %collective-permute-start.12 = (bf16[64,1664]{1,0:T(8,128)(2,1)}, bf16[64,1664]{1,0:T(8,128)(2,1)S(1)}, u32[]{:S(2)}, u32[]{:S(2)}) collective-permute-start(bf16[64,1664]{1,0:T(8,128)(2,1)} %all_gather.7), channel_id=1, source_target_pairs={{0,480},{32,0},{64,32},{96,64},{128,96},{160,128},{192,160},{224,1... | collective-permute-start | bytes 638984 | tf_op jit(solution)/shard_map/ppermute | solution.py:23
  135.6 2.3 %collective-permute-start.17 = (bf16[64,1664]{1,0:T(8,128)(2,1)}, bf16[64,1664]{1,0:T(8,128)(2,1)S(1)}, u32[]{:S(2)}, u32[]{:S(2)}) collective-permute-start(bf16[64,1664]{1,0:T(8,128)(2,1)} %collective-permute-done.11), channel_id=1, source_target_pairs={{0,32},{32,64},{64,96},{96,128},{128,160},{160,192},{192,224},{224... | collective-permute-start | bytes 638984 | tf_op jit(solution)/shard_map/ppermute | solution.py:23
  137.9 4.5 %collective-permute-start.15 = (bf16[64,1664]{1,0:T(8,128)(2,1)}, bf16[64,1664]{1,0:T(8,128)(2,1)S(1)}, u32[]{:S(2)}, u32[]{:S(2)}) collective-permute-start(bf16[64,1664]{1,0:T(8,128)(2,1)} %collective-permute-done.11), channel_id=1, source_target_pairs={{0,64},{32,480},{64,128},{96,32},{128,192},{160,96},{192,256},{224... | collective-permute-start | bytes 638984 | tf_op jit(solution)/shard_map/ppermute | solution.py:27
  143.8 4.6 %collective-permute-start.13 = (bf16[64,1664]{1,0:T(8,128)(2,1)}, bf16[64,1664]{1,0:T(8,128)(2,1)S(1)}, u32[]{:S(2)}, u32[]{:S(2)}) collective-permute-start(bf16[64,1664]{1,0:T(8,128)(2,1)} %collective-permute-done.11), channel_id=1, source_target_pairs={{0,480},{32,0},{64,32},{96,64},{128,96},{160,128},{192,160},{224,1... | collective-permute-start | bytes 638984 | tf_op jit(solution)/shard_map/ppermute | solution.py:23
  154.5 6.9 %all-to-all-start.1 = ((bf16[16,32,512]{2,1,0:T(8,128)(2,1)}), bf16[16,32,512]{2,1,0:T(8,128)(2,1)S(1)}, u32[]{:S(2)}, u32[]{:S(2)}) async-start(bf16[16,32,512]{2,1,0:T(8,128)(2,1)} %maximum_maximum_fusion), calls=%async_computation.1 | async-start | bytes 1048576 | tf_op jit(solution)/shard_map/all_to_all | solution.py:132
  161.4 9.4 %all-to-all-done.1 = bf16[16,32,512]{2,1,0:T(8,128)(2,1)S(1)} async-done(((bf16[16,32,512]{2,1,0:T(8,128)(2,1)}), bf16[16,32,512]{2,1,0:T(8,128)(2,1)S(1)}, u32[]{:S(2)}, u32[]{:S(2)}) %all-to-all-start.1) | async-done | bytes 524320 | tf_op jit(solution)/shard_map/all_to_all | solution.py:132
  (60 shorter events, 24.0 us)
Async XLA Ops:
  0.0 32.0 %copy-start = (bf16[512,1664]{1,0:T(8,128)(2,1)S(1)}, bf16[512,1664]{1,0:T(8,128)(2,1)}, u32[]{:S(2)}) copy-start(bf16[512,1664]{1,0:T(8,128)(2,1)} %param.6) | copy-start | bytes 5111812
  0.0 21.9 %copy-start.2 = (bf16[512,1664]{1,0:T(8,128)(2,1)S(1)}, bf16[512,1664]{1,0:T(8,128)(2,1)}, u32[]{:S(2)}) copy-start(bf16[512,1664]{1,0:T(8,128)(2,1)} %param.7) | copy-start | bytes 5111812
  1.6 12.2 %all-to-all-start = ((bf16[8,32,512]{2,1,0:T(8,128)(2,1)}), bf16[8,32,512]{2,1,0:T(8,128)(2,1)}, u32[]{:S(2)}, u32[]{:S(2)}) async-start(bf16[8,32,512]{2,1,0:T(8,128)(2,1)} %broadcast_in_dim.2), calls=%async_computation | async-start | bytes 524288 | tf_op jit(solution)/shard_map/all_to_all | solution.py:66
  22.3 18.4 %collective-permute-start.4 = (bf16[128,1664]{1,0:T(8,128)(2,1)S(1)}, bf16[128,1664]{1,0:T(8,128)(2,1)S(1)}, u32[]{:S(2)}, u32[]{:S(2)}) collective-permute-start(bf16[128,1664]{1,0:T(8,128)(2,1)S(1)} %convolution_convert_fusion.4), channel_id=1, source_target_pairs={{0,32},{32,64},{64,96},{96,128},{128,160},{160,192},{192,224},{224... | collective-permute-start | bytes 1277960 | tf_op jit(solution)/shard_map/ppermute | solution.py:23
  24.7 16.0 %collective-permute-start.5 = (bf16[128,1664]{1,0:T(8,128)(2,1)S(1)}, bf16[128,1664]{1,0:T(8,128)(2,1)S(1)}, u32[]{:S(2)}, u32[]{:S(2)}) collective-permute-start(bf16[128,1664]{1,0:T(8,128)(2,1)S(1)} %convolution_convert_fusion.3), channel_id=1, source_target_pairs={{0,480},{32,0},{64,32},{96,64},{128,96},{160,128},{192,160},{224,1... | collective-permute-start | bytes 1277960 | tf_op jit(solution)/shard_map/ppermute | solution.py:23
  32.8 24.6 %collective-permute-start = (bf16[256,1792]{1,0:T(8,128)(2,1)S(1)}, bf16[256,1792]{1,0:T(8,128)(2,1)S(1)}, u32[]{:S(2)}, u32[]{:S(2)}) collective-permute-start(bf16[256,1792]{1,0:T(8,128)(2,1)S(1)} %pad_maximum_fusion), channel_id=1, source_target_pairs={{0,16},{16,0},{1,17},{17,1},{2,18},{18,2},{3,19},{19,3},{4,20},{20... | collective-permute-start | bytes 2752520 | tf_op jit(solution)/shard_map/ppermute | solution.py:31
  37.6 14.4 %collective-permute-start.6 = (bf16[128,1664]{1,0:T(8,128)(2,1)S(1)}, bf16[128,1664]{1,0:T(8,128)(2,1)S(1)}, u32[]{:S(2)}, u32[]{:S(2)}) collective-permute-start(bf16[128,1664]{1,0:T(8,128)(2,1)S(1)} %convolution_convert_fusion.2), channel_id=1, source_target_pairs={{0,64},{32,480},{64,128},{96,32},{128,192},{160,96},{192,256},{224... | collective-permute-start | bytes 1277960 | tf_op jit(solution)/shard_map/ppermute | solution.py:27
  52.5 14.0 %collective-permute-start.7 = (bf16[64,1664]{1,0:T(8,128)(2,1)S(1)}, bf16[64,1664]{1,0:T(8,128)(2,1)S(1)}, u32[]{:S(2)}, u32[]{:S(2)}) collective-permute-start(bf16[64,1664]{1,0:T(8,128)(2,1)S(1)} %fusion.6), channel_id=1, source_target_pairs={{0,16},{16,0},{1,17},{17,1},{2,18},{18,2},{3,19},{19,3},{4,20},{20... | collective-permute-start | bytes 638984 | tf_op jit(solution)/shard_map/ppermute | solution.py:31
  57.7 8.9 %collective-permute-start.1 = (bf16[64,1792]{1,0:T(8,128)(2,1)S(1)}, bf16[64,1792]{1,0:T(8,128)(2,1)S(1)}, u32[]{:S(2)}, u32[]{:S(2)}) collective-permute-start(bf16[64,1792]{1,0:T(8,128)(2,1)S(1)} %get-tuple-element.17), channel_id=1, source_target_pairs={{0,32},{32,64},{64,96},{96,128},{128,160},{160,192},{192,224},{224... | collective-permute-start | bytes 688136 | tf_op jit(solution)/shard_map/ppermute | solution.py:23
  59.6 11.6 %collective-permute-start.3 = (bf16[64,1792]{1,0:T(8,128)(2,1)S(1)}, bf16[64,1792]{1,0:T(8,128)(2,1)S(1)}, u32[]{:S(2)}, u32[]{:S(2)}) collective-permute-start(bf16[64,1792]{1,0:T(8,128)(2,1)S(1)} %get-tuple-element.18), channel_id=1, source_target_pairs={{0,64},{32,480},{64,128},{96,32},{128,192},{160,96},{192,256},{224... | collective-permute-start | bytes 688136 | tf_op jit(solution)/shard_map/ppermute | solution.py:27
  61.5 30.9 %copy-start.3 = (s32[1664]{0:T(1024)S(1)}, s32[1664]{0:T(1024)}, u32[]{:S(2)}) copy-start(s32[1664]{0:T(1024)} %param.9) | copy-start | bytes 19972
  61.5 12.5 %collective-permute-start.2 = (bf16[64,1792]{1,0:T(8,128)(2,1)S(1)}, bf16[64,1792]{1,0:T(8,128)(2,1)S(1)}, u32[]{:S(2)}, u32[]{:S(2)}) collective-permute-start(bf16[64,1792]{1,0:T(8,128)(2,1)S(1)} %get-tuple-element.19), channel_id=1, source_target_pairs={{0,480},{32,0},{64,32},{96,64},{128,96},{160,128},{192,160},{224,1... | collective-permute-start | bytes 688136 | tf_op jit(solution)/shard_map/ppermute | solution.py:23
  66.5 75.9 %copy-start.1 = (bf16[1664,512]{1,0:T(8,128)(2,1)S(1)}, bf16[1664,512]{1,0:T(8,128)(2,1)}, u32[]{:S(2)}) copy-start(bf16[1664,512]{1,0:T(8,128)(2,1)} %param.8) | copy-start | bytes 5111812
  74.3 18.2 %collective-permute-start.10 = (bf16[16,3456]{1,0:T(8,128)(2,1)S(1)}, bf16[16,3456]{1,0:T(8,128)(2,1)S(1)}, u32[]{:S(2)}, u32[]{:S(2)}) collective-permute-start(bf16[16,3456]{1,0:T(8,128)(2,1)S(1)} %get-tuple-element.26), channel_id=1, source_target_pairs={{0,256},{32,288},{64,320},{96,352},{128,384},{160,416},{192,448},{... | collective-permute-start | bytes 331784 | tf_op jit(solution)/shard_map/ppermute | solution.py:23
  83.2 17.9 %collective-permute-start.9 = (bf16[16,3456]{1,0:T(8,128)(2,1)S(1)}, bf16[16,3456]{1,0:T(8,128)(2,1)S(1)}, u32[]{:S(2)}, u32[]{:S(2)}) collective-permute-start(bf16[16,3456]{1,0:T(8,128)(2,1)S(1)} %get-tuple-element.27), channel_id=1, source_target_pairs={{0,384},{32,416},{64,448},{96,480},{128,0},{160,32},{192,64},{224,... | collective-permute-start | bytes 331784 | tf_op jit(solution)/shard_map/ppermute | solution.py:23
  85.1 15.9 %collective-permute-start.8 = (bf16[16,3456]{1,0:T(8,128)(2,1)S(1)}, bf16[16,3456]{1,0:T(8,128)(2,1)S(1)}, u32[]{:S(2)}, u32[]{:S(2)}) collective-permute-start(bf16[16,3456]{1,0:T(8,128)(2,1)S(1)} %get-tuple-element.28), channel_id=1, source_target_pairs={{0,128},{32,160},{64,192},{96,224},{128,256},{160,288},{192,320},{... | collective-permute-start | bytes 331784 | tf_op jit(solution)/shard_map/ppermute | solution.py:23
  120.2 15.4 %collective-permute-start.11 = (bf16[64,1664]{1,0:T(8,128)(2,1)}, bf16[64,1664]{1,0:T(8,128)(2,1)}, u32[]{:S(2)}, u32[]{:S(2)}) collective-permute-start(bf16[64,1664]{1,0:T(8,128)(2,1)} %all_gather.7), channel_id=1, source_target_pairs={{0,16},{16,0},{1,17},{17,1},{2,18},{18,2},{3,19},{19,3},{4,20},{20... | collective-permute-start | bytes 638984 | tf_op jit(solution)/shard_map/ppermute | solution.py:31
  126.4 17.4 %collective-permute-start.16 = (bf16[64,1664]{1,0:T(8,128)(2,1)}, bf16[64,1664]{1,0:T(8,128)(2,1)S(1)}, u32[]{:S(2)}, u32[]{:S(2)}) collective-permute-start(bf16[64,1664]{1,0:T(8,128)(2,1)} %all_gather.7), channel_id=1, source_target_pairs={{0,32},{32,64},{64,96},{96,128},{128,160},{160,192},{192,224},{224... | collective-permute-start | bytes 638984 | tf_op jit(solution)/shard_map/ppermute | solution.py:23
  128.3 20.5 %collective-permute-start.14 = (bf16[64,1664]{1,0:T(8,128)(2,1)}, bf16[64,1664]{1,0:T(8,128)(2,1)S(1)}, u32[]{:S(2)}, u32[]{:S(2)}) collective-permute-start(bf16[64,1664]{1,0:T(8,128)(2,1)} %all_gather.7), channel_id=1, source_target_pairs={{0,64},{32,480},{64,128},{96,32},{128,192},{160,96},{192,256},{224... | collective-permute-start | bytes 638984 | tf_op jit(solution)/shard_map/ppermute | solution.py:27
  130.9 19.7 %collective-permute-start.12 = (bf16[64,1664]{1,0:T(8,128)(2,1)}, bf16[64,1664]{1,0:T(8,128)(2,1)S(1)}, u32[]{:S(2)}, u32[]{:S(2)}) collective-permute-start(bf16[64,1664]{1,0:T(8,128)(2,1)} %all_gather.7), channel_id=1, source_target_pairs={{0,480},{32,0},{64,32},{96,64},{128,96},{160,128},{192,160},{224,1... | collective-permute-start | bytes 638984 | tf_op jit(solution)/shard_map/ppermute | solution.py:23
  135.6 15.4 %collective-permute-start.17 = (bf16[64,1664]{1,0:T(8,128)(2,1)}, bf16[64,1664]{1,0:T(8,128)(2,1)S(1)}, u32[]{:S(2)}, u32[]{:S(2)}) collective-permute-start(bf16[64,1664]{1,0:T(8,128)(2,1)} %collective-permute-done.11), channel_id=1, source_target_pairs={{0,32},{32,64},{64,96},{96,128},{128,160},{160,192},{192,224},{224... | collective-permute-start | bytes 638984 | tf_op jit(solution)/shard_map/ppermute | solution.py:23
  137.9 13.5 %collective-permute-start.15 = (bf16[64,1664]{1,0:T(8,128)(2,1)}, bf16[64,1664]{1,0:T(8,128)(2,1)S(1)}, u32[]{:S(2)}, u32[]{:S(2)}) collective-permute-start(bf16[64,1664]{1,0:T(8,128)(2,1)} %collective-permute-done.11), channel_id=1, source_target_pairs={{0,64},{32,480},{64,128},{96,32},{128,192},{160,96},{192,256},{224... | collective-permute-start | bytes 638984 | tf_op jit(solution)/shard_map/ppermute | solution.py:27
  143.8 9.4 %collective-permute-start.13 = (bf16[64,1664]{1,0:T(8,128)(2,1)}, bf16[64,1664]{1,0:T(8,128)(2,1)S(1)}, u32[]{:S(2)}, u32[]{:S(2)}) collective-permute-start(bf16[64,1664]{1,0:T(8,128)(2,1)} %collective-permute-done.11), channel_id=1, source_target_pairs={{0,480},{32,0},{64,32},{96,64},{128,96},{160,128},{192,160},{224,1... | collective-permute-start | bytes 638984 | tf_op jit(solution)/shard_map/ppermute | solution.py:23
  154.5 16.3 %all-to-all-start.1 = ((bf16[16,32,512]{2,1,0:T(8,128)(2,1)}), bf16[16,32,512]{2,1,0:T(8,128)(2,1)S(1)}, u32[]{:S(2)}, u32[]{:S(2)}) async-start(bf16[16,32,512]{2,1,0:T(8,128)(2,1)} %maximum_maximum_fusion), calls=%async_computation.1 | async-start | bytes 1048576 | tf_op jit(solution)/shard_map/all_to_all | solution.py:132

commit v4 on v3

--- a/solution.py
+++ b/solution.py
@@ -83,11 +83,11 @@
 
     up1 = up_of(1, tokens)
     up_c = along_z(up1, 1)
-    up3 = up_of(3, up1)
+    gate_out = gate_of(1 - xh, up1).astype(bf16)
+    gate_in = across_x(gate_out)
+    up3 = up_of(3, gate_out)
     up_d = along_z(up3, -1)
-    gate_out = gate_of(1 - xh, up3).astype(bf16)
-    gate_in = across_x(gate_out)
-    up2 = up_of(2, gate_out)
+    up2 = up_of(2, up3)
     up_a = two_along_z(up2)
     up_own = up_of(0, up2).astype(f32)
     gate_own = gate_of(xh, up2)
@@ -116,22 +116,18 @@
         compiler_params=pltpu.CompilerParams(vmem_limit_bytes=4 * 1024 * 1024),
     )(pick(both, zh, 0), far_a, far_b, far_c, sign_bits.reshape(1, UNITS))
 
-    mine = lax.all_gather(rotated, "zh", axis=0, tiled=True)
-    theirs = across_x(mine)
+    far = lax.all_gather(rotated, "zh", axis=0, tiled=True)
+    near = lax.all_gather(far, "xh", axis=0, tiled=True)
+    n3 = along_z(near, 1)
+    n1 = along_z(near, -1)
+    n2 = jnp.concatenate([along_z(n1[:64], -1), along_z(n3[64:], 1)], axis=0)
 
-    def from_near(v):
-        return v, along_z(v, -1), two_along_z(v), along_z(v, 1)
+    def out_of(group):
+        pieces = [dot(v, down_weight).astype(bf16).reshape(16, 8, 512) for v in group]
+        parts = lax.all_to_all(jnp.concatenate(pieces, axis=1), ("c", "y", "xl"), 0, 0, tiled=True)
+        return jnp.sum(parts.astype(f32), axis=0).astype(bf16)
 
-    def out_of(v):
-        return dot(v, down_weight).astype(bf16).reshape(8, 8, 512)
-
-    own = [out_of(v) for v in from_near(mine)]
-    other = [out_of(v) for v in from_near(theirs)]
-    first = jnp.concatenate([jnp.where(xh == 0, p, q) for p, q in zip(own, other)], axis=1)
-    second = jnp.concatenate([jnp.where(xh == 0, q, p) for p, q in zip(own, other)], axis=1)
-    parts = lax.all_to_all(jnp.concatenate([first, second], axis=0), ("c", "y", "xl"), 0, 0, tiled=True)
-    out = jnp.sum(parts.astype(f32), axis=0).astype(bf16)
-
+    out = jnp.concatenate([out_of(group) for group in ((near, n1, n2, n3),)], axis=0)
     out = jnp.concatenate([out, out], axis=0)
     return lax.dynamic_slice_in_dim(out, ((4 - zl) & 3) * 8, 32, 0)
 

time: 172 us -> 170 us (0.988)
  starting transfers between devices: 84.2 us -> 73.3 us
  waiting for transfers between devices: 47.4 us -> 56.9 us
  matrix products: 8.14 us -> 4.61 us
  blocking collectives: 26.8 us -> 30 us
    ppermute x11, waiting for transfers between devices: 13.4 us -> 24.4 us  [along_z(): return lax.ppermute(x, Z, [(i, (i + d) % 16) for i in range(16)])]
    ppermute x3 -> x2, starting transfers between devices: 13 us -> 4.47 us  [across_x(): return lax.ppermute(x, 'xh', [(0, 1), (1, 0)])]
    ppermute x4 -> x2, starting transfers between devices: 10.9 us -> 5.69 us  [two_along_z(): lax.ppermute(x, Z, [(i, (i + (-2 if i % 2 else 2)) % 16) for i in range(1...]
    dot_general x14 -> x10, matrix products: 8.14 us -> 4.61 us  [dot(): return jnp.dot(a, b, preferred_element_type=f32)]
    all_gather x1 -> x2, blocking collectives: 18.8 us -> 21.9 us  [the longest x1 15.1 us: local(): far = lax.all_gather(rotated, 'zh', axis=0, tiled=True)]
    all_to_all x1, starting transfers between devices: 6.85 us -> 9.5 us  [out_of(): lax.all_to_all(jnp.concatenate(pieces, axis=1), ('c', 'y', 'xl'), 0, 0, t...]
    ppermute x3 -> x2, waiting for transfers between devices: 2.53 us -> 0.01 us  [across_x(): return lax.ppermute(x, 'xh', [(0, 1), (1, 0)])]
    ppermute x4 -> x2, waiting for transfers between devices: 15.9 us -> 16.9 us  [two_along_z(): lax.ppermute(x, Z, [(i, (i + (-2 if i % 2 else 2)) % 16) for i in range(1...]
  transfers between devices with their start and end apart: 20 -> 17, of which waited for: 9 -> 11; matrix products, arithmetic and copies ran while one was open for 5% -> 3% of each run, Pallas kernels for 0% -> 0%
where the time goes in v4:
time: 170 us
  starting transfers between devices  73.3 us (43%)
  waiting for transfers between devices  56.9 us (33%)
  blocking collectives  30 us (18%)
  matrix products  4.61 us (3%)
  other arithmetic  2.21 us (1%)
  local copies, waits for them, and re-layouts  1.93 us (1%)
    ppermute x11, starting transfers between devices, along_z(): return lax.ppermute(x, Z, [(i, (i + d) % 16) for i in range(16)])  47.7 us
    ppermute x11, waiting for transfers between devices, along_z(): return lax.ppermute(x, Z, [(i, (i + d) % 16) for i in range(16)])  24.4 us
    ppermute x2, waiting for transfers between devices, two_along_z(): lax.ppermute(x, Z, [(i, (i + (-2 if i % 2 else 2)) % 16) for i in range(1...  16.9 us
    all_gather x1, blocking collectives, local(): far = lax.all_gather(rotated, 'zh', axis=0, tiled=True)  15.1 us
    all_to_all x1, starting transfers between devices, out_of(): lax.all_to_all(jnp.concatenate(pieces, axis=1), ('c', 'y', 'xl'), 0, 0, t...  9.5 us
    all_to_all x1, waiting for transfers between devices, out_of(): lax.all_to_all(jnp.concatenate(pieces, axis=1), ('c', 'y', 'xl'), 0, 0, t...  9.4 us
    all_gather x1, blocking collectives, local(): gathered = lax.all_gather(some, 'c', axis=0, tiled=True)  8.07 us
    all_gather x1, blocking collectives, local(): near = lax.all_gather(far, 'xh', axis=0, tiled=True)  6.86 us
  transfers between devices with their start and end apart: 17, of which 11 were waited for; matrix products, arithmetic and copies ran while one was open for 3% of the time, Pallas kernels for 0%

profile of v4, /device:TPU:1, one launch (start us, length us, event | category | flops | bytes accessed | tf_op | source)
XLA Modules:
  0.0 169.7 jit_solution(6968545618217038036)
XLA Ops:
  1.6 5.9 %all-to-all-start = ((bf16[8,32,512]{2,1,0:T(8,128)(2,1)}), bf16[8,32,512]{2,1,0:T(8,128)(2,1)}, u32[]{:S(2)}, u32[]{:S(2)}) async-start(bf16[8,32,512]{2,1,0:T(8,128)(2,1)} %broadcast_in_dim.2), calls=%async_computation | async-start | bytes 524288 | tf_op jit(solution)/shard_map/all_to_all | solution.py:66
  7.6 6.2 %all-to-all-done = bf16[8,32,512]{2,1,0:T(8,128)(2,1)} async-done(((bf16[8,32,512]{2,1,0:T(8,128)(2,1)}), bf16[8,32,512]{2,1,0:T(8,128)(2,1)}, u32[]{:S(2)}, u32[]{:S(2)}) %all-to-all-start) | async-done | bytes 262176 | tf_op jit(solution)/shard_map/all_to_all | solution.py:66
  13.8 8.1 %all_gather.9 = bf16[512,512]{1,0:T(8,128)(2,1)S(1)} all-gather(bf16[256,512]{1,0:T(8,128)(2,1)} %bitcast), channel_id=1, replica_groups=mesh['zh'=4,'zl'=4,'xh'=2,'y'=4,'xl'=2,'c'=2] {'c'}, dimensions={0}, use_global_device_ids=true | all-gather | bytes 786432 | tf_op jit(solution)/shard_map/all_gather | solution.py:67
  27.6 9.5 %collective-permute-start.5 = (bf16[128,1664]{1,0:T(8,128)(2,1)S(1)}, bf16[128,1664]{1,0:T(8,128)(2,1)S(1)}, u32[]{:S(2)}, u32[]{:S(2)}) collective-permute-start(bf16[128,1664]{1,0:T(8,128)(2,1)S(1)} %convolution_convert_fusion.3), channel_id=1, source_target_pairs={{0,480},{32,0},{64,32},{96,64},{128,96},{160,128},{192,160},{224,1... | collective-permute-start | bytes 1277960 | tf_op jit(solution)/shard_map/ppermute | solution.py:23
  40.3 11.7 %collective-permute-done.6 = bf16[128,1664]{1,0:T(8,128)(2,1)S(1)} collective-permute-done((bf16[128,1664]{1,0:T(8,128)(2,1)S(1)}, bf16[128,1664]{1,0:T(8,128)(2,1)S(1)}, u32[]{:S(2)}, u32[]{:S(2)}) %collective-permute-start.6) | collective-permute-done | bytes 426016 | tf_op jit(solution)/shard_map/ppermute | solution.py:27
  52.0 2.8 %collective-permute-done.5 = bf16[128,1664]{1,0:T(8,128)(2,1)S(1)} collective-permute-done((bf16[128,1664]{1,0:T(8,128)(2,1)S(1)}, bf16[128,1664]{1,0:T(8,128)(2,1)S(1)}, u32[]{:S(2)}, u32[]{:S(2)}) %collective-permute-start.5) | collective-permute-done | bytes 426016 | tf_op jit(solution)/shard_map/ppermute | solution.py:23
  55.2 2.4 %collective-permute-start.7 = (bf16[64,1664]{1,0:T(8,128)(2,1)S(1)}, bf16[64,1664]{1,0:T(8,128)(2,1)S(1)}, u32[]{:S(2)}, u32[]{:S(2)}) collective-permute-start(bf16[64,1664]{1,0:T(8,128)(2,1)S(1)} %fusion.13), channel_id=1, source_target_pairs={{0,16},{16,0},{1,17},{17,1},{2,18},{18,2},{3,19},{19,3},{4,20},{20... | collective-permute-start | bytes 638984 | tf_op jit(solution)/shard_map/ppermute | solution.py:31
  59.9 3.8 %collective-permute-start.3 = (bf16[64,1792]{1,0:T(8,128)(2,1)S(1)}, bf16[64,1792]{1,0:T(8,128)(2,1)S(1)}, u32[]{:S(2)}, u32[]{:S(2)}) collective-permute-start(bf16[64,1792]{1,0:T(8,128)(2,1)S(1)} %get-tuple-element.18), channel_id=1, source_target_pairs={{0,64},{32,480},{64,128},{96,32},{128,192},{160,96},{192,256},{224... | collective-permute-start | bytes 688136 | tf_op jit(solution)/shard_map/ppermute | solution.py:27
  63.6 4.3 %collective-permute-start.2 = (bf16[64,1792]{1,0:T(8,128)(2,1)S(1)}, bf16[64,1792]{1,0:T(8,128)(2,1)S(1)}, u32[]{:S(2)}, u32[]{:S(2)}) collective-permute-start(bf16[64,1792]{1,0:T(8,128)(2,1)S(1)} %get-tuple-element.19), channel_id=1, source_target_pairs={{0,480},{32,0},{64,32},{96,64},{128,96},{160,128},{192,160},{224,1... | collective-permute-start | bytes 688136 | tf_op jit(solution)/shard_map/ppermute | solution.py:23
  68.0 5.2 %collective-permute-done.3 = bf16[64,1792]{1,0:T(8,128)(2,1)S(1)} collective-permute-done((bf16[64,1792]{1,0:T(8,128)(2,1)S(1)}, bf16[64,1792]{1,0:T(8,128)(2,1)S(1)}, u32[]{:S(2)}, u32[]{:S(2)}) %collective-permute-start.3) | collective-permute-done | bytes 229408 | tf_op jit(solution)/shard_map/ppermute | solution.py:27
  73.2 2.1 %collective-permute-done.2 = bf16[64,1792]{1,0:T(8,128)(2,1)S(1)} collective-permute-done((bf16[64,1792]{1,0:T(8,128)(2,1)S(1)}, bf16[64,1792]{1,0:T(8,128)(2,1)S(1)}, u32[]{:S(2)}, u32[]{:S(2)}) %collective-permute-start.2) | collective-permute-done | bytes 229408 | tf_op jit(solution)/shard_map/ppermute | solution.py:23
  75.5 7.4 %collective-permute-start.10 = (bf16[16,3456]{1,0:T(8,128)(2,1)S(1)}, bf16[16,3456]{1,0:T(8,128)(2,1)S(1)}, u32[]{:S(2)}, u32[]{:S(2)}) collective-permute-start(bf16[16,3456]{1,0:T(8,128)(2,1)S(1)} %get-tuple-element.26), channel_id=1, source_target_pairs={{0,256},{32,288},{64,320},{96,352},{128,384},{160,416},{192,448},{... | collective-permute-start | bytes 331784 | tf_op jit(solution)/shard_map/ppermute | solution.py:23
  82.9 2.7 %collective-permute-start.9 = (bf16[16,3456]{1,0:T(8,128)(2,1)S(1)}, bf16[16,3456]{1,0:T(8,128)(2,1)S(1)}, u32[]{:S(2)}, u32[]{:S(2)}) collective-permute-start(bf16[16,3456]{1,0:T(8,128)(2,1)S(1)} %get-tuple-element.27), channel_id=1, source_target_pairs={{0,384},{32,416},{64,448},{96,480},{128,0},{160,32},{192,64},{224,... | collective-permute-start | bytes 331784 | tf_op jit(solution)/shard_map/ppermute | solution.py:23
  85.7 6.4 %collective-permute-start.8 = (bf16[16,3456]{1,0:T(8,128)(2,1)S(1)}, bf16[16,3456]{1,0:T(8,128)(2,1)S(1)}, u32[]{:S(2)}, u32[]{:S(2)}) collective-permute-start(bf16[16,3456]{1,0:T(8,128)(2,1)S(1)} %get-tuple-element.28), channel_id=1, source_target_pairs={{0,128},{32,160},{64,192},{96,224},{128,256},{160,288},{192,320},{... | collective-permute-start | bytes 331784 | tf_op jit(solution)/shard_map/ppermute | solution.py:23
  92.2 2.4 %collective-permute-done.10.c = bf16[16,3456]{1,0:T(8,128)(2,1)S(1)} collective-permute-done((bf16[16,3456]{1,0:T(8,128)(2,1)S(1)}, bf16[16,3456]{1,0:T(8,128)(2,1)S(1)}, u32[]{:S(2)}, u32[]{:S(2)}) %collective-permute-start.10) | collective-permute-done | bytes 110624 | tf_op jit(solution)/shard_map/ppermute | solution.py:23
  94.6 9.4 %collective-permute-done.9.b = bf16[16,3456]{1,0:T(8,128)(2,1)S(1)} collective-permute-done((bf16[16,3456]{1,0:T(8,128)(2,1)S(1)}, bf16[16,3456]{1,0:T(8,128)(2,1)S(1)}, u32[]{:S(2)}, u32[]{:S(2)}) %collective-permute-start.9) | collective-permute-done | bytes 110624 | tf_op jit(solution)/shard_map/ppermute | solution.py:23
  104.3 15.1 %all_gather.10 = bf16[64,1664]{1,0:T(8,128)(2,1)S(1)} all-gather(bf16[16,1664]{1,0:T(8,128)(2,1)S(1)} %shard_map.55), channel_id=1, replica_groups=mesh['zh'=4,'zl'=4,'xh'=2,'y'=4,'xl'=2,'c'=2] {'zh'}, dimensions={0}, use_global_device_ids=true | all-gather | bytes 266240 | tf_op jit(solution)/shard_map/all_gather | solution.py:119
  119.3 6.9 %all_gather.11 = bf16[128,1664]{1,0:T(8,128)(2,1)S(1)} all-gather(bf16[64,1664]{1,0:T(8,128)(2,1)S(1)} %all_gather.10), channel_id=1, replica_groups=mesh['zh'=4,'zl'=4,'xh'=2,'y'=4,'xl'=2,'c'=2] {'xh'}, dimensions={0}, use_global_device_ids=true | all-gather | bytes 638976 | tf_op jit(solution)/shard_map/all_gather | solution.py:120
  126.2 5.1 %collective-permute-start.13 = (bf16[128,1664]{1,0:T(8,128)(2,1)S(1)}, bf16[128,1664]{1,0:T(8,128)(2,1)S(1)}, u32[]{:S(2)}, u32[]{:S(2)}) collective-permute-start(bf16[128,1664]{1,0:T(8,128)(2,1)S(1)} %all_gather.11), channel_id=1, source_target_pairs={{0,32},{32,64},{64,96},{96,128},{128,160},{160,192},{192,224},{224... | collective-permute-start | bytes 1277960 | tf_op jit(solution)/shard_map/ppermute | solution.py:23
  133.7 3.1 %collective-permute-done.13 = bf16[128,1664]{1,0:T(8,128)(2,1)S(1)} collective-permute-done((bf16[128,1664]{1,0:T(8,128)(2,1)S(1)}, bf16[128,1664]{1,0:T(8,128)(2,1)S(1)}, u32[]{:S(2)}, u32[]{:S(2)}) %collective-permute-start.13) | collective-permute-done | bytes 426016 | tf_op jit(solution)/shard_map/ppermute | solution.py:23
  136.9 4.5 %collective-permute-start.14 = (bf16[64,1664]{1,0:T(8,128)(2,1)S(1)}, bf16[64,1664]{1,0:T(8,128)(2,1)S(1)}, u32[]{:S(2)}, u32[]{:S(2)}) collective-permute-start(bf16[64,1664]{1,0:T(8,128)(2,1)S(1)} %slice.49), channel_id=1, source_target_pairs={{0,32},{32,64},{64,96},{96,128},{128,160},{160,192},{192,224},{224... | collective-permute-start | bytes 638984 | tf_op jit(solution)/shard_map/ppermute | solution.py:23
  144.9 3.9 %collective-permute-done.12 = bf16[64,1664]{1,0:T(8,128)(2,1)S(1)} collective-permute-done((bf16[64,1664]{1,0:T(8,128)(2,1)S(1)}, bf16[64,1664]{1,0:T(8,128)(2,1)S(1)}, u32[]{:S(2)}, u32[]{:S(2)}) %collective-permute-start.12) | collective-permute-done | bytes 213024 | tf_op jit(solution)/shard_map/ppermute | solution.py:23
  150.1 9.5 %all-to-all-start.1 = ((bf16[16,32,512]{2,1,0:T(8,128)(2,1)}), bf16[16,32,512]{2,1,0:T(8,128)(2,1)S(1)}, u32[]{:S(2)}, u32[]{:S(2)}) async-start(bf16[16,32,512]{2,1,0:T(8,128)(2,1)} %pad_maximum_fusion.1), calls=%async_computation.1 | async-start | bytes 1048576 | tf_op jit(solution)/shard_map/all_to_all | solution.py:127
  159.6 9.4 %all-to-all-done.1 = bf16[16,32,512]{2,1,0:T(8,128)(2,1)S(1)} async-done(((bf16[16,32,512]{2,1,0:T(8,128)(2,1)}), bf16[16,32,512]{2,1,0:T(8,128)(2,1)S(1)}, u32[]{:S(2)}, u32[]{:S(2)}) %all-to-all-start.1) | async-done | bytes 524320 | tf_op jit(solution)/shard_map/all_to_all | solution.py:127
  (53 shorter events, 21.5 us)
Async XLA Ops:
  0.0 24.4 %copy-start = (bf16[512,1664]{1,0:T(8,128)(2,1)S(1)}, bf16[512,1664]{1,0:T(8,128)(2,1)}, u32[]{:S(2)}) copy-start(bf16[512,1664]{1,0:T(8,128)(2,1)} %param.6) | copy-start | bytes 5111812
  0.0 21.9 %copy-start.2 = (bf16[512,1664]{1,0:T(8,128)(2,1)S(1)}, bf16[512,1664]{1,0:T(8,128)(2,1)}, u32[]{:S(2)}) copy-start(bf16[512,1664]{1,0:T(8,128)(2,1)} %param.7) | copy-start | bytes 5111812
  1.6 12.2 %all-to-all-start = ((bf16[8,32,512]{2,1,0:T(8,128)(2,1)}), bf16[8,32,512]{2,1,0:T(8,128)(2,1)}, u32[]{:S(2)}, u32[]{:S(2)}) async-start(bf16[8,32,512]{2,1,0:T(8,128)(2,1)} %broadcast_in_dim.2), calls=%async_computation | async-start | bytes 524288 | tf_op jit(solution)/shard_map/all_to_all | solution.py:66
  22.4 17.9 %collective-permute-start.4 = (bf16[128,1664]{1,0:T(8,128)(2,1)S(1)}, bf16[128,1664]{1,0:T(8,128)(2,1)S(1)}, u32[]{:S(2)}, u32[]{:S(2)}) collective-permute-start(bf16[128,1664]{1,0:T(8,128)(2,1)S(1)} %convolution_convert_fusion.4), channel_id=1, source_target_pairs={{0,32},{32,64},{64,96},{96,128},{128,160},{160,192},{192,224},{224... | collective-permute-start | bytes 1277960 | tf_op jit(solution)/shard_map/ppermute | solution.py:23
  25.2 32.5 %collective-permute-start = (bf16[256,1792]{1,0:T(8,128)(2,1)S(1)}, bf16[256,1792]{1,0:T(8,128)(2,1)S(1)}, u32[]{:S(2)}, u32[]{:S(2)}) collective-permute-start(bf16[256,1792]{1,0:T(8,128)(2,1)S(1)} %pad_maximum_fusion), channel_id=1, source_target_pairs={{0,16},{16,0},{1,17},{17,1},{2,18},{18,2},{3,19},{19,3},{4,20},{20... | collective-permute-start | bytes 2752520 | tf_op jit(solution)/shard_map/ppermute | solution.py:31
  27.6 27.1 %collective-permute-start.5 = (bf16[128,1664]{1,0:T(8,128)(2,1)S(1)}, bf16[128,1664]{1,0:T(8,128)(2,1)S(1)}, u32[]{:S(2)}, u32[]{:S(2)}) collective-permute-start(bf16[128,1664]{1,0:T(8,128)(2,1)S(1)} %convolution_convert_fusion.3), channel_id=1, source_target_pairs={{0,480},{32,0},{64,32},{96,64},{128,96},{160,128},{192,160},{224,1... | collective-permute-start | bytes 1277960 | tf_op jit(solution)/shard_map/ppermute | solution.py:23
  37.6 14.4 %collective-permute-start.6 = (bf16[128,1664]{1,0:T(8,128)(2,1)S(1)}, bf16[128,1664]{1,0:T(8,128)(2,1)S(1)}, u32[]{:S(2)}, u32[]{:S(2)}) collective-permute-start(bf16[128,1664]{1,0:T(8,128)(2,1)S(1)} %convolution_convert_fusion.2), channel_id=1, source_target_pairs={{0,64},{32,480},{64,128},{96,32},{128,192},{160,96},{192,256},{224... | collective-permute-start | bytes 1277960 | tf_op jit(solution)/shard_map/ppermute | solution.py:27
  55.2 12.7 %collective-permute-start.7 = (bf16[64,1664]{1,0:T(8,128)(2,1)S(1)}, bf16[64,1664]{1,0:T(8,128)(2,1)S(1)}, u32[]{:S(2)}, u32[]{:S(2)}) collective-permute-start(bf16[64,1664]{1,0:T(8,128)(2,1)S(1)} %fusion.13), channel_id=1, source_target_pairs={{0,16},{16,0},{1,17},{17,1},{2,18},{18,2},{3,19},{19,3},{4,20},{20... | collective-permute-start | bytes 638984 | tf_op jit(solution)/shard_map/ppermute | solution.py:31
  57.9 10.1 %collective-permute-start.1 = (bf16[64,1792]{1,0:T(8,128)(2,1)S(1)}, bf16[64,1792]{1,0:T(8,128)(2,1)S(1)}, u32[]{:S(2)}, u32[]{:S(2)}) collective-permute-start(bf16[64,1792]{1,0:T(8,128)(2,1)S(1)} %get-tuple-element.17), channel_id=1, source_target_pairs={{0,32},{32,64},{64,96},{96,128},{128,160},{160,192},{192,224},{224... | collective-permute-start | bytes 688136 | tf_op jit(solution)/shard_map/ppermute | solution.py:23
  59.9 13.3 %collective-permute-start.3 = (bf16[64,1792]{1,0:T(8,128)(2,1)S(1)}, bf16[64,1792]{1,0:T(8,128)(2,1)S(1)}, u32[]{:S(2)}, u32[]{:S(2)}) collective-permute-start(bf16[64,1792]{1,0:T(8,128)(2,1)S(1)} %get-tuple-element.18), channel_id=1, source_target_pairs={{0,64},{32,480},{64,128},{96,32},{128,192},{160,96},{192,256},{224... | collective-permute-start | bytes 688136 | tf_op jit(solution)/shard_map/ppermute | solution.py:27
  63.6 28.5 %copy-start.3 = (s32[1664]{0:T(1024)S(1)}, s32[1664]{0:T(1024)}, u32[]{:S(2)}) copy-start(s32[1664]{0:T(1024)} %param.9) | copy-start | bytes 19972
  63.6 11.6 %collective-permute-start.2 = (bf16[64,1792]{1,0:T(8,128)(2,1)S(1)}, bf16[64,1792]{1,0:T(8,128)(2,1)S(1)}, u32[]{:S(2)}, u32[]{:S(2)}) collective-permute-start(bf16[64,1792]{1,0:T(8,128)(2,1)S(1)} %get-tuple-element.19), channel_id=1, source_target_pairs={{0,480},{32,0},{64,32},{96,64},{128,96},{160,128},{192,160},{224,1... | collective-permute-start | bytes 688136 | tf_op jit(solution)/shard_map/ppermute | solution.py:23
  75.4 57.9 %copy-start.1 = (bf16[1664,512]{1,0:T(8,128)(2,1)S(1)}, bf16[1664,512]{1,0:T(8,128)(2,1)}, u32[]{:S(2)}) copy-start(bf16[1664,512]{1,0:T(8,128)(2,1)} %param.8) | copy-start | bytes 5111812
  75.5 19.0 %collective-permute-start.10 = (bf16[16,3456]{1,0:T(8,128)(2,1)S(1)}, bf16[16,3456]{1,0:T(8,128)(2,1)S(1)}, u32[]{:S(2)}, u32[]{:S(2)}) collective-permute-start(bf16[16,3456]{1,0:T(8,128)(2,1)S(1)} %get-tuple-element.26), channel_id=1, source_target_pairs={{0,256},{32,288},{64,320},{96,352},{128,384},{160,416},{192,448},{... | collective-permute-start | bytes 331784 | tf_op jit(solution)/shard_map/ppermute | solution.py:23
  82.9 21.0 %collective-permute-start.9 = (bf16[16,3456]{1,0:T(8,128)(2,1)S(1)}, bf16[16,3456]{1,0:T(8,128)(2,1)S(1)}, u32[]{:S(2)}, u32[]{:S(2)}) collective-permute-start(bf16[16,3456]{1,0:T(8,128)(2,1)S(1)} %get-tuple-element.27), channel_id=1, source_target_pairs={{0,384},{32,416},{64,448},{96,480},{128,0},{160,32},{192,64},{224,... | collective-permute-start | bytes 331784 | tf_op jit(solution)/shard_map/ppermute | solution.py:23
  85.7 18.3 %collective-permute-start.8 = (bf16[16,3456]{1,0:T(8,128)(2,1)S(1)}, bf16[16,3456]{1,0:T(8,128)(2,1)S(1)}, u32[]{:S(2)}, u32[]{:S(2)}) collective-permute-start(bf16[16,3456]{1,0:T(8,128)(2,1)S(1)} %get-tuple-element.28), channel_id=1, source_target_pairs={{0,128},{32,160},{64,192},{96,224},{128,256},{160,288},{192,320},{... | collective-permute-start | bytes 331784 | tf_op jit(solution)/shard_map/ppermute | solution.py:23
  126.2 10.7 %collective-permute-start.13 = (bf16[128,1664]{1,0:T(8,128)(2,1)S(1)}, bf16[128,1664]{1,0:T(8,128)(2,1)S(1)}, u32[]{:S(2)}, u32[]{:S(2)}) collective-permute-start(bf16[128,1664]{1,0:T(8,128)(2,1)S(1)} %all_gather.11), channel_id=1, source_target_pairs={{0,32},{32,64},{64,96},{96,128},{128,160},{160,192},{192,224},{224... | collective-permute-start | bytes 1277960 | tf_op jit(solution)/shard_map/ppermute | solution.py:23
  131.3 10.8 %collective-permute-start.11 = (bf16[128,1664]{1,0:T(8,128)(2,1)S(1)}, bf16[128,1664]{1,0:T(8,128)(2,1)S(1)}, u32[]{:S(2)}, u32[]{:S(2)}) collective-permute-start(bf16[128,1664]{1,0:T(8,128)(2,1)S(1)} %all_gather.11), channel_id=1, source_target_pairs={{0,480},{32,0},{64,32},{96,64},{128,96},{160,128},{192,160},{224,1... | collective-permute-start | bytes 1277960 | tf_op jit(solution)/shard_map/ppermute | solution.py:23
  136.9 8.1 %collective-permute-start.14 = (bf16[64,1664]{1,0:T(8,128)(2,1)S(1)}, bf16[64,1664]{1,0:T(8,128)(2,1)S(1)}, u32[]{:S(2)}, u32[]{:S(2)}) collective-permute-start(bf16[64,1664]{1,0:T(8,128)(2,1)S(1)} %slice.49), channel_id=1, source_target_pairs={{0,32},{32,64},{64,96},{96,128},{128,160},{160,192},{192,224},{224... | collective-permute-start | bytes 638984 | tf_op jit(solution)/shard_map/ppermute | solution.py:23
  142.2 6.6 %collective-permute-start.12 = (bf16[64,1664]{1,0:T(8,128)(2,1)S(1)}, bf16[64,1664]{1,0:T(8,128)(2,1)S(1)}, u32[]{:S(2)}, u32[]{:S(2)}) collective-permute-start(bf16[64,1664]{1,0:T(8,128)(2,1)S(1)} %slice.48), channel_id=1, source_target_pairs={{0,480},{32,0},{64,32},{96,64},{128,96},{160,128},{192,160},{224,1... | collective-permute-start | bytes 638984 | tf_op jit(solution)/shard_map/ppermute | solution.py:23
  150.1 18.9 %all-to-all-start.1 = ((bf16[16,32,512]{2,1,0:T(8,128)(2,1)}), bf16[16,32,512]{2,1,0:T(8,128)(2,1)S(1)}, u32[]{:S(2)}, u32[]{:S(2)}) async-start(bf16[16,32,512]{2,1,0:T(8,128)(2,1)} %pad_maximum_fusion.1), calls=%async_computation.1 | async-start | bytes 1048576 | tf_op jit(solution)/shard_map/all_to_all | solution.py:127

commit v5 on v4

--- a/solution.py
+++ b/solution.py
@@ -83,11 +83,11 @@
 
     up1 = up_of(1, tokens)
     up_c = along_z(up1, 1)
-    gate_out = gate_of(1 - xh, up1).astype(bf16)
+    up3 = up_of(3, up1)
+    up_d = along_z(up3, -1)
+    gate_out = gate_of(1 - xh, up3).astype(bf16)
     gate_in = across_x(gate_out)
-    up3 = up_of(3, gate_out)
-    up_d = along_z(up3, -1)
-    up2 = up_of(2, up3)
+    up2 = up_of(2, gate_out)
     up_a = two_along_z(up2)
     up_own = up_of(0, up2).astype(f32)
     gate_own = gate_of(xh, up2)

time: 170 us -> 173 us (1.018)
  blocking collectives: 30 us -> 34.4 us
  waiting for transfers between devices: 56.9 us -> 53.3 us
    ppermute x11, waiting for transfers between devices: 24.4 us -> 19.2 us  [along_z(): return lax.ppermute(x, Z, [(i, (i + d) % 16) for i in range(16)])]
    all_gather x1, blocking collectives: 15.1 us -> 18 us  [local(): far = lax.all_gather(rotated, 'zh', axis=0, tiled=True)]
    ppermute x2, waiting for transfers between devices: 0.01 us -> 2.53 us  [across_x(): return lax.ppermute(x, 'xh', [(0, 1), (1, 0)])]
    ppermute x2, starting transfers between devices: 4.47 us -> 6.79 us  [across_x(): return lax.ppermute(x, 'xh', [(0, 1), (1, 0)])]
    ppermute x2, starting transfers between devices: 5.69 us -> 3.84 us  [two_along_z(): lax.ppermute(x, Z, [(i, (i + (-2 if i % 2 else 2)) % 16) for i in range(1...]
  transfers between devices with their start and end apart: 17 -> 17, of which waited for: 11 -> 12; matrix products, arithmetic and copies ran while one was open for 3% -> 3% of each run, Pallas kernels for 0% -> 0%
where the time goes in v5:
time: 173 us; the launch traced here: 172 us
  starting transfers between devices  74.9 us (43%)
  waiting for transfers between devices  53.3 us (31%)
  blocking collectives  34.4 us (20%)
  matrix products  4.61 us (3%)
  other arithmetic  2.2 us (1%)
  local copies, waits for them, and re-layouts  1.93 us (1%)
    ppermute x11, starting transfers between devices, along_z(): return lax.ppermute(x, Z, [(i, (i + d) % 16) for i in range(16)])  47.1 us
    ppermute x11, waiting for transfers between devices, along_z(): return lax.ppermute(x, Z, [(i, (i + d) % 16) for i in range(16)])  19.2 us
    all_gather x1, blocking collectives, local(): far = lax.all_gather(rotated, 'zh', axis=0, tiled=True)  18 us
    ppermute x2, waiting for transfers between devices, two_along_z(): lax.ppermute(x, Z, [(i, (i + (-2 if i % 2 else 2)) % 16) for i in range(1...  15.9 us
    all_to_all x1, starting transfers between devices, out_of(): lax.all_to_all(jnp.concatenate(pieces, axis=1), ('c', 'y', 'xl'), 0, 0, t...  11.2 us
    all_to_all x1, waiting for transfers between devices, out_of(): lax.all_to_all(jnp.concatenate(pieces, axis=1), ('c', 'y', 'xl'), 0, 0, t...  9.4 us
    all_gather x1, blocking collectives, local(): near = lax.all_gather(far, 'xh', axis=0, tiled=True)  8.33 us
    all_gather x1, blocking collectives, local(): gathered = lax.all_gather(some, 'c', axis=0, tiled=True)  8.07 us
  transfers between devices with their start and end apart: 17, of which 12 were waited for; matrix products, arithmetic and copies ran while one was open for 3% of the time, Pallas kernels for 0%

profile of v5, /device:TPU:1, one launch (start us, length us, event | category | flops | bytes accessed | tf_op | source)
XLA Modules:
  0.0 172.0 jit_solution(1045155634105314748)
XLA Ops:
  1.6 5.9 %all-to-all-start = ((bf16[8,32,512]{2,1,0:T(8,128)(2,1)}), bf16[8,32,512]{2,1,0:T(8,128)(2,1)}, u32[]{:S(2)}, u32[]{:S(2)}) async-start(bf16[8,32,512]{2,1,0:T(8,128)(2,1)} %broadcast_in_dim.2), calls=%async_computation | async-start | bytes 524288 | tf_op jit(solution)/shard_map/all_to_all | solution.py:66
  7.6 6.2 %all-to-all-done = bf16[8,32,512]{2,1,0:T(8,128)(2,1)} async-done(((bf16[8,32,512]{2,1,0:T(8,128)(2,1)}), bf16[8,32,512]{2,1,0:T(8,128)(2,1)}, u32[]{:S(2)}, u32[]{:S(2)}) %all-to-all-start) | async-done | bytes 262176 | tf_op jit(solution)/shard_map/all_to_all | solution.py:66
  13.8 8.1 %all_gather.9 = bf16[512,512]{1,0:T(8,128)(2,1)S(1)} all-gather(bf16[256,512]{1,0:T(8,128)(2,1)} %bitcast), channel_id=1, replica_groups=mesh['zh'=4,'zl'=4,'xh'=2,'y'=4,'xl'=2,'c'=2] {'c'}, dimensions={0}, use_global_device_ids=true | all-gather | bytes 786432 | tf_op jit(solution)/shard_map/all_gather | solution.py:67
  24.7 7.2 %collective-permute-start.5 = (bf16[128,1664]{1,0:T(8,128)(2,1)S(1)}, bf16[128,1664]{1,0:T(8,128)(2,1)S(1)}, u32[]{:S(2)}, u32[]{:S(2)}) collective-permute-start(bf16[128,1664]{1,0:T(8,128)(2,1)S(1)} %convolution_convert_fusion.3), channel_id=1, source_target_pairs={{0,480},{32,0},{64,32},{96,64},{128,96},{160,128},{192,160},{224,1... | collective-permute-start | bytes 1277960 | tf_op jit(solution)/shard_map/ppermute | solution.py:23
  32.8 4.4 %collective-permute-start = (bf16[256,1792]{1,0:T(8,128)(2,1)S(1)}, bf16[256,1792]{1,0:T(8,128)(2,1)S(1)}, u32[]{:S(2)}, u32[]{:S(2)}) collective-permute-start(bf16[256,1792]{1,0:T(8,128)(2,1)S(1)} %pad_maximum_fusion), channel_id=1, source_target_pairs={{0,16},{16,0},{1,17},{17,1},{2,18},{18,2},{3,19},{19,3},{4,20},{20... | collective-permute-start | bytes 2752520 | tf_op jit(solution)/shard_map/ppermute | solution.py:31
  40.7 11.2 %collective-permute-done.6 = bf16[128,1664]{1,0:T(8,128)(2,1)S(1)} collective-permute-done((bf16[128,1664]{1,0:T(8,128)(2,1)S(1)}, bf16[128,1664]{1,0:T(8,128)(2,1)S(1)}, u32[]{:S(2)}, u32[]{:S(2)}) %collective-permute-start.6) | collective-permute-done | bytes 426016 | tf_op jit(solution)/shard_map/ppermute | solution.py:27
  52.5 2.4 %collective-permute-start.7 = (bf16[64,1664]{1,0:T(8,128)(2,1)S(1)}, bf16[64,1664]{1,0:T(8,128)(2,1)S(1)}, u32[]{:S(2)}, u32[]{:S(2)}) collective-permute-start(bf16[64,1664]{1,0:T(8,128)(2,1)S(1)} %fusion.13), channel_id=1, source_target_pairs={{0,16},{16,0},{1,17},{17,1},{2,18},{18,2},{3,19},{19,3},{4,20},{20... | collective-permute-start | bytes 638984 | tf_op jit(solution)/shard_map/ppermute | solution.py:31
  54.9 2.5 %collective-permute-done = bf16[256,1792]{1,0:T(8,128)(2,1)S(1)} collective-permute-done((bf16[256,1792]{1,0:T(8,128)(2,1)S(1)}, bf16[256,1792]{1,0:T(8,128)(2,1)S(1)}, u32[]{:S(2)}, u32[]{:S(2)}) %collective-permute-start) | collective-permute-done | bytes 917536 | tf_op jit(solution)/shard_map/ppermute | solution.py:31
  57.6 1.9 %collective-permute-start.1 = (bf16[64,1792]{1,0:T(8,128)(2,1)S(1)}, bf16[64,1792]{1,0:T(8,128)(2,1)S(1)}, u32[]{:S(2)}, u32[]{:S(2)}) collective-permute-start(bf16[64,1792]{1,0:T(8,128)(2,1)S(1)} %get-tuple-element.17), channel_id=1, source_target_pairs={{0,32},{32,64},{64,96},{96,128},{128,160},{160,192},{192,224},{224... | collective-permute-start | bytes 688136 | tf_op jit(solution)/shard_map/ppermute | solution.py:23
  61.5 4.9 %collective-permute-start.2 = (bf16[64,1792]{1,0:T(8,128)(2,1)S(1)}, bf16[64,1792]{1,0:T(8,128)(2,1)S(1)}, u32[]{:S(2)}, u32[]{:S(2)}) collective-permute-start(bf16[64,1792]{1,0:T(8,128)(2,1)S(1)} %get-tuple-element.19), channel_id=1, source_target_pairs={{0,480},{32,0},{64,32},{96,64},{128,96},{160,128},{192,160},{224,1... | collective-permute-start | bytes 688136 | tf_op jit(solution)/shard_map/ppermute | solution.py:23
  66.5 4.6 %collective-permute-done.3 = bf16[64,1792]{1,0:T(8,128)(2,1)S(1)} collective-permute-done((bf16[64,1792]{1,0:T(8,128)(2,1)S(1)}, bf16[64,1792]{1,0:T(8,128)(2,1)S(1)}, u32[]{:S(2)}, u32[]{:S(2)}) %collective-permute-start.3) | collective-permute-done | bytes 229408 | tf_op jit(solution)/shard_map/ppermute | solution.py:27
  71.1 2.9 %collective-permute-done.2 = bf16[64,1792]{1,0:T(8,128)(2,1)S(1)} collective-permute-done((bf16[64,1792]{1,0:T(8,128)(2,1)S(1)}, bf16[64,1792]{1,0:T(8,128)(2,1)S(1)}, u32[]{:S(2)}, u32[]{:S(2)}) %collective-permute-start.2) | collective-permute-done | bytes 229408 | tf_op jit(solution)/shard_map/ppermute | solution.py:23
  74.3 9.1 %collective-permute-start.10 = (bf16[16,3456]{1,0:T(8,128)(2,1)S(1)}, bf16[16,3456]{1,0:T(8,128)(2,1)S(1)}, u32[]{:S(2)}, u32[]{:S(2)}) collective-permute-start(bf16[16,3456]{1,0:T(8,128)(2,1)S(1)} %get-tuple-element.26), channel_id=1, source_target_pairs={{0,256},{32,288},{64,320},{96,352},{128,384},{160,416},{192,448},{... | collective-permute-start | bytes 331784 | tf_op jit(solution)/shard_map/ppermute | solution.py:23
  85.3 7.3 %collective-permute-start.8 = (bf16[16,3456]{1,0:T(8,128)(2,1)S(1)}, bf16[16,3456]{1,0:T(8,128)(2,1)S(1)}, u32[]{:S(2)}, u32[]{:S(2)}) collective-permute-start(bf16[16,3456]{1,0:T(8,128)(2,1)S(1)} %get-tuple-element.28), channel_id=1, source_target_pairs={{0,128},{32,160},{64,192},{96,224},{128,256},{160,288},{192,320},{... | collective-permute-start | bytes 331784 | tf_op jit(solution)/shard_map/ppermute | solution.py:23
  92.6 8.5 %collective-permute-done.9.b = bf16[16,3456]{1,0:T(8,128)(2,1)S(1)} collective-permute-done((bf16[16,3456]{1,0:T(8,128)(2,1)S(1)}, bf16[16,3456]{1,0:T(8,128)(2,1)S(1)}, u32[]{:S(2)}, u32[]{:S(2)}) %collective-permute-start.9) | collective-permute-done | bytes 110624 | tf_op jit(solution)/shard_map/ppermute | solution.py:23
  101.5 18.0 %all_gather.10 = bf16[64,1664]{1,0:T(8,128)(2,1)S(1)} all-gather(bf16[16,1664]{1,0:T(8,128)(2,1)S(1)} %shard_map.55), channel_id=1, replica_groups=mesh['zh'=4,'zl'=4,'xh'=2,'y'=4,'xl'=2,'c'=2] {'zh'}, dimensions={0}, use_global_device_ids=true | all-gather | bytes 266240 | tf_op jit(solution)/shard_map/all_gather | solution.py:119
  119.5 8.3 %all_gather.11 = bf16[128,1664]{1,0:T(8,128)(2,1)S(1)} all-gather(bf16[64,1664]{1,0:T(8,128)(2,1)S(1)} %all_gather.10), channel_id=1, replica_groups=mesh['zh'=4,'zl'=4,'xh'=2,'y'=4,'xl'=2,'c'=2] {'xh'}, dimensions={0}, use_global_device_ids=true | all-gather | bytes 638976 | tf_op jit(solution)/shard_map/all_gather | solution.py:120
  127.8 4.8 %collective-permute-start.13 = (bf16[128,1664]{1,0:T(8,128)(2,1)S(1)}, bf16[128,1664]{1,0:T(8,128)(2,1)S(1)}, u32[]{:S(2)}, u32[]{:S(2)}) collective-permute-start(bf16[128,1664]{1,0:T(8,128)(2,1)S(1)} %all_gather.11), channel_id=1, source_target_pairs={{0,32},{32,64},{64,96},{96,128},{128,160},{160,192},{192,224},{224... | collective-permute-start | bytes 1277960 | tf_op jit(solution)/shard_map/ppermute | solution.py:23
  135.0 3.5 %collective-permute-done.13 = bf16[128,1664]{1,0:T(8,128)(2,1)S(1)} collective-permute-done((bf16[128,1664]{1,0:T(8,128)(2,1)S(1)}, bf16[128,1664]{1,0:T(8,128)(2,1)S(1)}, u32[]{:S(2)}, u32[]{:S(2)}) %collective-permute-start.13) | collective-permute-done | bytes 426016 | tf_op jit(solution)/shard_map/ppermute | solution.py:23
  138.5 3.0 %collective-permute-start.14 = (bf16[64,1664]{1,0:T(8,128)(2,1)S(1)}, bf16[64,1664]{1,0:T(8,128)(2,1)S(1)}, u32[]{:S(2)}, u32[]{:S(2)}) collective-permute-start(bf16[64,1664]{1,0:T(8,128)(2,1)S(1)} %slice.49), channel_id=1, source_target_pairs={{0,32},{32,64},{64,96},{96,128},{128,160},{160,192},{192,224},{224... | collective-permute-start | bytes 638984 | tf_op jit(solution)/shard_map/ppermute | solution.py:23
  141.8 3.2 %collective-permute-start.12 = (bf16[64,1664]{1,0:T(8,128)(2,1)S(1)}, bf16[64,1664]{1,0:T(8,128)(2,1)S(1)}, u32[]{:S(2)}, u32[]{:S(2)}) collective-permute-start(bf16[64,1664]{1,0:T(8,128)(2,1)S(1)} %slice.48), channel_id=1, source_target_pairs={{0,480},{32,0},{64,32},{96,64},{128,96},{160,128},{192,160},{224,1... | collective-permute-start | bytes 638984 | tf_op jit(solution)/shard_map/ppermute | solution.py:23
  146.3 3.1 %collective-permute-done.12 = bf16[64,1664]{1,0:T(8,128)(2,1)S(1)} collective-permute-done((bf16[64,1664]{1,0:T(8,128)(2,1)S(1)}, bf16[64,1664]{1,0:T(8,128)(2,1)S(1)}, u32[]{:S(2)}, u32[]{:S(2)}) %collective-permute-start.12) | collective-permute-done | bytes 213024 | tf_op jit(solution)/shard_map/ppermute | solution.py:23
  150.6 11.2 %all-to-all-start.1 = ((bf16[16,32,512]{2,1,0:T(8,128)(2,1)}), bf16[16,32,512]{2,1,0:T(8,128)(2,1)S(1)}, u32[]{:S(2)}, u32[]{:S(2)}) async-start(bf16[16,32,512]{2,1,0:T(8,128)(2,1)} %pad_maximum_fusion.1), calls=%async_computation.1 | async-start | bytes 1048576 | tf_op jit(solution)/shard_map/all_to_all | solution.py:127
  161.9 9.4 %all-to-all-done.1 = bf16[16,32,512]{2,1,0:T(8,128)(2,1)S(1)} async-done(((bf16[16,32,512]{2,1,0:T(8,128)(2,1)}), bf16[16,32,512]{2,1,0:T(8,128)(2,1)S(1)}, u32[]{:S(2)}, u32[]{:S(2)}) %all-to-all-start.1) | async-done | bytes 524320 | tf_op jit(solution)/shard_map/all_to_all | solution.py:127
  (53 shorter events, 19.8 us)
Async XLA Ops:
  0.0 32.0 %copy-start = (bf16[512,1664]{1,0:T(8,128)(2,1)S(1)}, bf16[512,1664]{1,0:T(8,128)(2,1)}, u32[]{:S(2)}) copy-start(bf16[512,1664]{1,0:T(8,128)(2,1)} %param.6) | copy-start | bytes 5111812
  0.0 21.9 %copy-start.2 = (bf16[512,1664]{1,0:T(8,128)(2,1)S(1)}, bf16[512,1664]{1,0:T(8,128)(2,1)}, u32[]{:S(2)}) copy-start(bf16[512,1664]{1,0:T(8,128)(2,1)} %param.7) | copy-start | bytes 5111812
  1.6 12.2 %all-to-all-start = ((bf16[8,32,512]{2,1,0:T(8,128)(2,1)}), bf16[8,32,512]{2,1,0:T(8,128)(2,1)}, u32[]{:S(2)}, u32[]{:S(2)}) async-start(bf16[8,32,512]{2,1,0:T(8,128)(2,1)} %broadcast_in_dim.2), calls=%async_computation | async-start | bytes 524288 | tf_op jit(solution)/shard_map/all_to_all | solution.py:66
  22.4 18.3 %collective-permute-start.4 = (bf16[128,1664]{1,0:T(8,128)(2,1)S(1)}, bf16[128,1664]{1,0:T(8,128)(2,1)S(1)}, u32[]{:S(2)}, u32[]{:S(2)}) collective-permute-start(bf16[128,1664]{1,0:T(8,128)(2,1)S(1)} %convolution_convert_fusion.4), channel_id=1, source_target_pairs={{0,32},{32,64},{64,96},{96,128},{128,160},{160,192},{192,224},{224... | collective-permute-start | bytes 1277960 | tf_op jit(solution)/shard_map/ppermute | solution.py:23
  24.7 16.0 %collective-permute-start.5 = (bf16[128,1664]{1,0:T(8,128)(2,1)S(1)}, bf16[128,1664]{1,0:T(8,128)(2,1)S(1)}, u32[]{:S(2)}, u32[]{:S(2)}) collective-permute-start(bf16[128,1664]{1,0:T(8,128)(2,1)S(1)} %convolution_convert_fusion.3), channel_id=1, source_target_pairs={{0,480},{32,0},{64,32},{96,64},{128,96},{160,128},{192,160},{224,1... | collective-permute-start | bytes 1277960 | tf_op jit(solution)/shard_map/ppermute | solution.py:23
  32.8 24.6 %collective-permute-start = (bf16[256,1792]{1,0:T(8,128)(2,1)S(1)}, bf16[256,1792]{1,0:T(8,128)(2,1)S(1)}, u32[]{:S(2)}, u32[]{:S(2)}) collective-permute-start(bf16[256,1792]{1,0:T(8,128)(2,1)S(1)} %pad_maximum_fusion), channel_id=1, source_target_pairs={{0,16},{16,0},{1,17},{17,1},{2,18},{18,2},{3,19},{19,3},{4,20},{20... | collective-permute-start | bytes 2752520 | tf_op jit(solution)/shard_map/ppermute | solution.py:31
  37.6 14.4 %collective-permute-start.6 = (bf16[128,1664]{1,0:T(8,128)(2,1)S(1)}, bf16[128,1664]{1,0:T(8,128)(2,1)S(1)}, u32[]{:S(2)}, u32[]{:S(2)}) collective-permute-start(bf16[128,1664]{1,0:T(8,128)(2,1)S(1)} %convolution_convert_fusion.2), channel_id=1, source_target_pairs={{0,64},{32,480},{64,128},{96,32},{128,192},{160,96},{192,256},{224... | collective-permute-start | bytes 1277960 | tf_op jit(solution)/shard_map/ppermute | solution.py:27
  52.5 14.0 %collective-permute-start.7 = (bf16[64,1664]{1,0:T(8,128)(2,1)S(1)}, bf16[64,1664]{1,0:T(8,128)(2,1)S(1)}, u32[]{:S(2)}, u32[]{:S(2)}) collective-permute-start(bf16[64,1664]{1,0:T(8,128)(2,1)S(1)} %fusion.13), channel_id=1, source_target_pairs={{0,16},{16,0},{1,17},{17,1},{2,18},{18,2},{3,19},{19,3},{4,20},{20... | collective-permute-start | bytes 638984 | tf_op jit(solution)/shard_map/ppermute | solution.py:31
  57.6 8.9 %collective-permute-start.1 = (bf16[64,1792]{1,0:T(8,128)(2,1)S(1)}, bf16[64,1792]{1,0:T(8,128)(2,1)S(1)}, u32[]{:S(2)}, u32[]{:S(2)}) collective-permute-start(bf16[64,1792]{1,0:T(8,128)(2,1)S(1)} %get-tuple-element.17), channel_id=1, source_target_pairs={{0,32},{32,64},{64,96},{96,128},{128,160},{160,192},{192,224},{224... | collective-permute-start | bytes 688136 | tf_op jit(solution)/shard_map/ppermute | solution.py:23
  59.6 11.6 %collective-permute-start.3 = (bf16[64,1792]{1,0:T(8,128)(2,1)S(1)}, bf16[64,1792]{1,0:T(8,128)(2,1)S(1)}, u32[]{:S(2)}, u32[]{:S(2)}) collective-permute-start(bf16[64,1792]{1,0:T(8,128)(2,1)S(1)} %get-tuple-element.18), channel_id=1, source_target_pairs={{0,64},{32,480},{64,128},{96,32},{128,192},{160,96},{192,256},{224... | collective-permute-start | bytes 688136 | tf_op jit(solution)/shard_map/ppermute | solution.py:27
  61.5 31.1 %copy-start.3 = (s32[1664]{0:T(1024)S(1)}, s32[1664]{0:T(1024)}, u32[]{:S(2)}) copy-start(s32[1664]{0:T(1024)} %param.9) | copy-start | bytes 19972
  61.5 12.5 %collective-permute-start.2 = (bf16[64,1792]{1,0:T(8,128)(2,1)S(1)}, bf16[64,1792]{1,0:T(8,128)(2,1)S(1)}, u32[]{:S(2)}, u32[]{:S(2)}) collective-permute-start(bf16[64,1792]{1,0:T(8,128)(2,1)S(1)} %get-tuple-element.19), channel_id=1, source_target_pairs={{0,480},{32,0},{64,32},{96,64},{128,96},{160,128},{192,160},{224,1... | collective-permute-start | bytes 688136 | tf_op jit(solution)/shard_map/ppermute | solution.py:23
  74.2 60.3 %copy-start.1 = (bf16[1664,512]{1,0:T(8,128)(2,1)S(1)}, bf16[1664,512]{1,0:T(8,128)(2,1)}, u32[]{:S(2)}) copy-start(bf16[1664,512]{1,0:T(8,128)(2,1)} %param.8) | copy-start | bytes 5111812
  74.3 18.3 %collective-permute-start.10 = (bf16[16,3456]{1,0:T(8,128)(2,1)S(1)}, bf16[16,3456]{1,0:T(8,128)(2,1)S(1)}, u32[]{:S(2)}, u32[]{:S(2)}) collective-permute-start(bf16[16,3456]{1,0:T(8,128)(2,1)S(1)} %get-tuple-element.26), channel_id=1, source_target_pairs={{0,256},{32,288},{64,320},{96,352},{128,384},{160,416},{192,448},{... | collective-permute-start | bytes 331784 | tf_op jit(solution)/shard_map/ppermute | solution.py:23
  83.4 17.8 %collective-permute-start.9 = (bf16[16,3456]{1,0:T(8,128)(2,1)S(1)}, bf16[16,3456]{1,0:T(8,128)(2,1)S(1)}, u32[]{:S(2)}, u32[]{:S(2)}) collective-permute-start(bf16[16,3456]{1,0:T(8,128)(2,1)S(1)} %get-tuple-element.27), channel_id=1, source_target_pairs={{0,384},{32,416},{64,448},{96,480},{128,0},{160,32},{192,64},{224,... | collective-permute-start | bytes 331784 | tf_op jit(solution)/shard_map/ppermute | solution.py:23
  85.3 15.9 %collective-permute-start.8 = (bf16[16,3456]{1,0:T(8,128)(2,1)S(1)}, bf16[16,3456]{1,0:T(8,128)(2,1)S(1)}, u32[]{:S(2)}, u32[]{:S(2)}) collective-permute-start(bf16[16,3456]{1,0:T(8,128)(2,1)S(1)} %get-tuple-element.28), channel_id=1, source_target_pairs={{0,128},{32,160},{64,192},{96,224},{128,256},{160,288},{192,320},{... | collective-permute-start | bytes 331784 | tf_op jit(solution)/shard_map/ppermute | solution.py:23
  127.8 10.7 %collective-permute-start.13 = (bf16[128,1664]{1,0:T(8,128)(2,1)S(1)}, bf16[128,1664]{1,0:T(8,128)(2,1)S(1)}, u32[]{:S(2)}, u32[]{:S(2)}) collective-permute-start(bf16[128,1664]{1,0:T(8,128)(2,1)S(1)} %all_gather.11), channel_id=1, source_target_pairs={{0,32},{32,64},{64,96},{96,128},{128,160},{160,192},{192,224},{224... | collective-permute-start | bytes 1277960 | tf_op jit(solution)/shard_map/ppermute | solution.py:23
  132.6 9.2 %collective-permute-start.11 = (bf16[128,1664]{1,0:T(8,128)(2,1)S(1)}, bf16[128,1664]{1,0:T(8,128)(2,1)S(1)}, u32[]{:S(2)}, u32[]{:S(2)}) collective-permute-start(bf16[128,1664]{1,0:T(8,128)(2,1)S(1)} %all_gather.11), channel_id=1, source_target_pairs={{0,480},{32,0},{64,32},{96,64},{128,96},{160,128},{192,160},{224,1... | collective-permute-start | bytes 1277960 | tf_op jit(solution)/shard_map/ppermute | solution.py:23
  138.5 7.8 %collective-permute-start.14 = (bf16[64,1664]{1,0:T(8,128)(2,1)S(1)}, bf16[64,1664]{1,0:T(8,128)(2,1)S(1)}, u32[]{:S(2)}, u32[]{:S(2)}) collective-permute-start(bf16[64,1664]{1,0:T(8,128)(2,1)S(1)} %slice.49), channel_id=1, source_target_pairs={{0,32},{32,64},{64,96},{96,128},{128,160},{160,192},{192,224},{224... | collective-permute-start | bytes 638984 | tf_op jit(solution)/shard_map/ppermute | solution.py:23
  141.8 7.6 %collective-permute-start.12 = (bf16[64,1664]{1,0:T(8,128)(2,1)S(1)}, bf16[64,1664]{1,0:T(8,128)(2,1)S(1)}, u32[]{:S(2)}, u32[]{:S(2)}) collective-permute-start(bf16[64,1664]{1,0:T(8,128)(2,1)S(1)} %slice.48), channel_id=1, source_target_pairs={{0,480},{32,0},{64,32},{96,64},{128,96},{160,128},{192,160},{224,1... | collective-permute-start | bytes 638984 | tf_op jit(solution)/shard_map/ppermute | solution.py:23
  150.6 20.6 %all-to-all-start.1 = ((bf16[16,32,512]{2,1,0:T(8,128)(2,1)}), bf16[16,32,512]{2,1,0:T(8,128)(2,1)S(1)}, u32[]{:S(2)}, u32[]{:S(2)}) async-start(bf16[16,32,512]{2,1,0:T(8,128)(2,1)} %pad_maximum_fusion.1), calls=%async_computation.1 | async-start | bytes 1048576 | tf_op jit(solution)/shard_map/all_to_all | solution.py:127
